TPU v7x, 256 devices: a whole 4x4x8 slice. The times are simulated.
256 devices in a mesh: shot: 16 (over x, y_lo, core), space: 16 (over y_hi, z).
Axes of the slice: x: 4, y: 4 (y_hi: 2, y_lo: 2; y = y_hi * 2 + y_lo), z: 8, core: 2. Of those that a mesh axis runs over, the one named last changes fastest.
Arguments:
- courant: float32 [256, 64, 256], P('space'), may hold values from 0.05 to 0.18
- snapshot_store: bfloat16 [256, 2, 16, 64, 256], P('shot', None, 'space'), may hold values from -6 to 6
- slab_holder: int32 [16, 16], replicated, may hold values from 0 to 255, as said below
- snap_step: int32 [16], P('shot'), may hold values from 0 to 55
- window_end: int32 [16], P('shot'), may hold values from 2 to 63, as said below
- source_cell: int32 [16], P('shot'), may hold values from 0 to 4194303
- wavelet: float32 [64], replicated, may hold values from -6 to 6
- receiver_cells: int32 [16, 256], P('shot'), may hold values from 0 to 4194303
- residual_data: float32 [16, 3, 256], P('shot'), may hold values from -6 to 6
- adjoint_prev: float32 [16, 256, 64, 256], P('shot', 'space'), may hold values from -6 to 6
- adjoint_now: float32 [16, 256, 64, 256], P('shot', 'space'), may hold values from -6 to 6
Outputs:
- image: float32 [256, 16384], P('space', 'shot')
- adjoint_out: float32 [16, 256, 64, 256], P('shot', 'space')
Inputs may be any that keep to these rules, and one draw needn't show every extreme that they name: `slab_holder`: every slot holds exactly one slab; a storing index s' holds exactly 2 slabs of a shot group or none, and slot // 16 is the storing index. window_end - snap_step lies between 2 and 8, and equals 8 for some shot group.
All inputs are finite; a program needn't handle non-finite values.
Results may differ from a plain program's by a relative error of at most 0.0003.
Values may be sent and summed in bfloat16 or wider, within the bound.
A program may use at most 128 MiB of HBM per device.

v0:
```python
import functools

import jax
import jax.numpy as jnp
from jax import lax
from jax.experimental import pallas as pl
from jax.experimental.pallas import tpu as pltpu
from jax.sharding import PartitionSpec as P

FWD = 8
ADJ = 3
HALO = 4
CAP = 2
SCALE = 5040.0
TAPS = (8064.0, -1008.0, 128.0, -9.0)
CENTRE_Z = -43008.0
CENTRE_Y = -42.0
CODE_BITS = 13.0
SCALE_ROWS = 16
MESH = pl.DeviceIdType.MESH
F32 = jnp.float32
BF16 = jnp.bfloat16


def band(size, block, centre):
    row = lax.broadcasted_iota(jnp.int32, (size, size), 0)
    col = lax.broadcasted_iota(jnp.int32, (size, size), 1)
    gap = jnp.abs(row - col)
    result = jnp.where(gap == 0, centre, 0.0)
    for offset, tap in enumerate(TAPS, 1):
        result = jnp.where(gap == offset, tap, result)
    if block < size:
        result = jnp.where(row // block == col // block, result, 0.0)
    return result.astype(BF16)


def split(value):
    high = value.astype(BF16)
    return high, (value - high.astype(F32)).astype(BF16)


def encode(value):
    rows = value.shape[0] * value.shape[1]
    flat = value.reshape(rows, value.shape[2])
    top = jnp.max(jnp.abs(flat), axis=0, keepdims=True)
    power = jnp.floor(jnp.log2(jnp.maximum(top, 1e-30)))
    code = jnp.round(flat * jnp.exp2(CODE_BITS - power)).astype(jnp.int32).astype(jnp.int16)
    scale = jnp.broadcast_to(power.astype(jnp.int32), (SCALE_ROWS, value.shape[2])).astype(jnp.int16)
    return code, scale


def decode(code, scale, shape):
    power = scale.astype(jnp.int32).astype(F32)[:1]
    return (code.astype(jnp.int32).astype(F32) * jnp.exp2(power - CODE_BITS)).reshape(shape)


def kernel(
    shots,
    spaces,
    cap,
    holder,
    snap_step,
    window_end,
    source_cell,
    wavelet,
    cells,
    residual,
    courant_in,
    store_in,
    prev_in,
    now_in,
    image_out,
    adjoint_out,
    courant,
    store,
    adj,
    field,
    wave,
    adj_code,
    adj_land,
    wave_code,
    wave_land,
    packed,
    landed,
    band_z,
    band_y,
    spot,
    col_hot,
    image,
    from_core,
    to_chip,
    from_chip,
    last,
    last_in,
    local_sem,
    fetch_send,
    fetch_recv,
    adj_send,
    adj_recv,
    wave_send,
    wave_recv,
    core_sem,
    chip_send,
    chip_recv,
    last_sem,
    out_sem,
):
    me = lax.axis_index("shot")
    place = lax.axis_index("space")
    planes, size_y, size_z = courant.shape
    slabs = store.shape[0]
    has_low = place > 0
    has_high = place < spaces - 1
    core = lax.rem(me, 2)
    chip = lax.div(me, 2)
    chips = shots // 2
    partner = chip * 2 + 1 - core
    half = planes // 2
    chunk = HALO
    chunks = planes // chunk
    inside = HALO

    def peer(shot):
        return (shot, place)

    loads = [
        pltpu.make_async_copy(now_in, adj.at[1], local_sem.at[0]),
        pltpu.make_async_copy(courant_in, courant, local_sem.at[1]),
        pltpu.make_async_copy(store_in, store, local_sem.at[2]),
        pltpu.make_async_copy(prev_in, adj.at[0], local_sem.at[3]),
    ]
    for load in loads:
        load.start()

    barrier = pltpu.get_barrier_semaphore()

    def greet(turn, carry):
        other = lax.rem(me + turn, shots)
        pl.semaphore_signal(barrier, inc=1, device_id=peer(other), device_id_type=MESH)
        return carry

    lax.fori_loop(1, shots, greet, 0)

    @pl.when(has_low)
    def _():
        pl.semaphore_signal(barrier, inc=1, device_id=(me, place - 1), device_id_type=MESH)

    @pl.when(has_high)
    def _():
        pl.semaphore_signal(barrier, inc=1, device_id=(me, place + 1), device_id_type=MESH)

    band_z[...] = band(size_z, size_z, CENTRE_Z)
    band_y[...] = band(chunk * size_y, size_y, CENTRE_Y)

    @pl.when(jnp.logical_not(has_low))
    def _():
        for slot in range(2):
            field[slot, :HALO] = jnp.zeros((HALO, size_y, size_z), F32)
            wave[slot, :HALO] = jnp.zeros((HALO, size_y, size_z), F32)

    @pl.when(jnp.logical_not(has_high))
    def _():
        for slot in range(2):
            field[slot, planes + HALO :] = jnp.zeros((HALO, size_y, size_z), F32)
            wave[slot, planes + HALO :] = jnp.zeros((HALO, size_y, size_z), F32)

    plane_cells = size_y * size_z
    source = source_cell[0]
    source_plane = lax.div(source, plane_cells) - place * planes
    in_plane = lax.rem(source, plane_cells)
    flat = lax.broadcasted_iota(jnp.int32, (size_y, size_z), 0) * size_z + lax.broadcasted_iota(
        jnp.int32, (size_y, size_z), 1
    )
    spot[...] = jnp.where(flat == in_plane, 1.0, 0.0)

    recv_cells = cells[...]
    recv_row = recv_cells // size_z - place * (planes * size_y)
    recv_col = recv_cells % size_z
    count = recv_cells.shape[1]
    col_hot[...] = jnp.where(
        lax.broadcasted_iota(jnp.int32, (size_z, count), 0) == recv_col, 1.0, 0.0
    ).astype(BF16)

    halo_rows = HALO * size_y
    edge_shape = (HALO, size_y, size_z)

    def halo_copy(code, land, slot, send, recv, side):
        return pltpu.make_async_remote_copy(
            src_ref=code.at[slot, side],
            dst_ref=land.at[slot, side],
            send_sem=send.at[slot, side],
            recv_sem=recv.at[slot, side],
            device_id=(me, place + 2 * side - 1),
            device_id_type=MESH,
        )

    has_side = (has_low, has_high)

    def halo_start(value, code, land, slot, send, recv, side):
        @pl.when(has_side[side])
        def _():
            numbers, scale = encode(value)
            code[slot, side, :halo_rows] = numbers
            code[slot, side, halo_rows:] = scale
            halo_copy(code, land, slot, send, recv, side).start()

    def halo_wait(ref, code, land, slot, send, recv, side):
        @pl.when(has_side[side])
        def _():
            halo_copy(code, land, slot, send, recv, side).wait_send()
            halo_copy(code, land, slot, send, recv, 1 - side).wait_recv()
            ref[slot, pl.ds((inside + planes) * side, HALO)] = decode(
                land[slot, 1 - side, :halo_rows], land[slot, 1 - side, halo_rows:], edge_shape
            )

    def stencil(ref, slot, index):
        first = inside + chunk * index
        middle = ref[slot, pl.ds(first, chunk)]
        high, low = split(middle.reshape(chunk * size_y, size_z))
        right = band_z[...]
        left = band_y[...]
        total = jnp.dot(high, right, preferred_element_type=F32)
        total += jnp.dot(low, right, preferred_element_type=F32)
        total += jnp.dot(left, high, preferred_element_type=F32)
        total += jnp.dot(left, low, preferred_element_type=F32)
        total = total.reshape(chunk, size_y, size_z)
        for offset, tap in enumerate(TAPS, 1):
            total += tap * (
                ref[slot, pl.ds(first + offset, chunk)] + ref[slot, pl.ds(first - offset, chunk)]
            )
        return total

    loads[0].wait()
    loads[1].wait()
    adj_halo = (adj_code, adj_land)
    adj_sems = (adj_send, adj_recv)
    wave_halo = (wave_code, wave_land)
    wave_sems = (wave_send, wave_recv)

    def first_field(index):
        part = pl.ds(chunk * index, chunk)
        scaled = courant[part] * (1.0 / SCALE)
        courant[part] = scaled
        value = scaled * adj[1, part]
        field[0, pl.ds(inside + chunk * index, chunk)] = value
        return value

    low_count = jnp.where(has_low, 1, 0)
    high_count = jnp.where(has_high, 1, 0)
    pl.semaphore_wait(barrier, shots - 1 + low_count + high_count)
    halo_start(first_field(0), *adj_halo, 0, *adj_sems, 0)
    halo_start(first_field(chunks - 1), *adj_halo, 0, *adj_sems, 1)

    def fetch_copy(level, other):
        return pltpu.make_async_remote_copy(
            src_ref=packed.at[level, pl.ds(other * cap, cap)],
            dst_ref=landed.at[level, pl.ds(me * cap, cap)],
            send_sem=fetch_send.at[level, other],
            recv_sem=fetch_recv.at[level, me],
            device_id=peer(other),
            device_id_type=MESH,
        )

    def fetch_arrival(level, other):
        return pltpu.make_async_remote_copy(
            src_ref=packed.at[level, pl.ds(other * cap, cap)],
            dst_ref=landed.at[level, pl.ds(other * cap, cap)],
            send_sem=fetch_send.at[level, other],
            recv_sem=fetch_recv.at[level, other],
            device_id=peer(other),
            device_id_type=MESH,
        )

    loads[2].wait()

    def held_for(other):
        found = jnp.int32(0)
        spots = [jnp.int32(0)] * cap
        for slab in range(slabs):
            slot = holder[other, slab]
            mine = lax.div(slot, slabs) == me
            where = lax.rem(slot, slabs)
            for rank in range(cap):
                spots[rank] = jnp.where(jnp.logical_and(mine, found == rank), where, spots[rank])
            found = found + jnp.where(mine, 1, 0)
        return spots

    def pack(turn, carry):
        other = lax.rem(me + turn, shots)
        spots = held_for(other)
        for rank in range(cap):
            for level in (1, 0):
                packed[level, other * cap + rank] = store[spots[rank], level]
        fetch_copy(1, other).start()
        return carry

    lax.fori_loop(1, shots, pack, 0)

    def send_older(turn, carry):
        fetch_copy(0, lax.rem(me + turn, shots)).start()
        return carry

    lax.fori_loop(1, shots, send_older, 0)
    own = held_for(me)
    for rank in range(cap):
        for level in (1, 0):
            landed[level, me * cap + rank] = store[own[rank], level]

    for index in range(1, chunks - 1):
        first_field(index)
    loads[3].wait()

    def adjoint_step(turn, carry):
        slot = lax.rem(turn, 2)
        data = residual[pl.ds(turn, 1)]
        data_high, data_low = split(data)
        data_high = data_high.astype(F32)
        data_low = data_low.astype(F32)
        hot = col_hot[...]

        def advance(index):
            part = pl.ds(chunk * index, chunk)
            row = lax.broadcasted_iota(jnp.int32, (chunk * size_y, count), 0) + (
                chunk * size_y * index
            )
            hit = row == recv_row
            total = lax.dot_general(
                jnp.where(hit, data_high, 0.0).astype(BF16),
                hot,
                (((1,), (1,)), ((), ())),
                preferred_element_type=F32,
            )
            total += lax.dot_general(
                jnp.where(hit, data_low, 0.0).astype(BF16),
                hot,
                (((1,), (1,)), ((), ())),
                preferred_element_type=F32,
            )
            total = total.reshape(chunk, size_y, size_z) + stencil(field, slot, index)
            current = adj[turn + 1, part]
            following = (current + current) - adj[turn, part] + total
            adj[turn + 2, part] = following
            value = courant[part] * following
            field[1 - slot, pl.ds(inside + chunk * index, chunk)] = value
            return value

        for side, index in ((0, 0), (1, chunks - 1)):
            halo_wait(field, *adj_halo, slot, *adj_sems, side)
            advance(index)

            @pl.when(turn < ADJ - 1)
            def _():
                value = field[1 - slot, pl.ds(inside + chunk * index, chunk)]
                halo_start(value, *adj_halo, 1 - slot, *adj_sems, side)

        for index in range(1, chunks - 1):
            advance(index)
        return carry

    lax.fori_loop(0, ADJ, adjoint_step, 0)
    result = pltpu.make_async_copy(adj.at[ADJ + 1], adjoint_out, out_sem.at[0])
    result.start()

    steps = window_end[0] - snap_step[0]
    idle = FWD - steps
    now_level = 1 - lax.rem(idle, 2)

    def arrive(turn, carry):
        other = lax.rem(me + turn, shots)
        for level in (1, 0):
            fetch_arrival(level, other).wait_recv()
        return carry

    lax.fori_loop(1, shots, arrive, 0)

    def unpack(slab, carry):
        storer = lax.div(holder[me, slab], slabs)
        rank = jnp.int32(0)
        for before in range(slabs):
            same = jnp.logical_and(lax.div(holder[me, before], slabs) == storer, before < slab)
            rank = rank + jnp.where(same, 1, 0)
        where = storer * cap + rank
        wave[0, inside + slab] = landed[now_level, where].astype(F32)
        wave[1, inside + slab] = landed[1 - now_level, where].astype(F32)
        return carry

    lax.fori_loop(0, slabs, unpack, 0)
    halo_start(wave[0, pl.ds(inside, HALO)], *wave_halo, 0, *wave_sems, 0)
    halo_start(wave[0, pl.ds(planes, HALO)], *wave_halo, 0, *wave_sems, 1)

    def forward_step(turn, carry):
        slot = lax.rem(turn, 2)
        moving = jnp.where(turn >= idle, 1.0, 0.0)
        amplitude = wavelet[snap_step[0] + jnp.maximum(turn - idle, 0)]

        def advance(index):
            part = pl.ds(chunk * index, chunk)
            padded = pl.ds(inside + chunk * index, chunk)
            total = courant[part] * stencil(wave, slot, index)
            gap = wave[slot, padded] - wave[1 - slot, padded]
            total = total + (gap + gap)
            pattern = spot[...]
            for plane in range(chunk):
                push = jnp.where(source_plane == chunk * index + plane, amplitude, 0.0)
                wave[1 - slot, inside + chunk * index + plane] = wave[
                    1 - slot, inside + chunk * index + plane
                ] + moving * (total[plane] + push * pattern)

        for side, index in ((0, 0), (1, chunks - 1)):
            halo_wait(wave, *wave_halo, slot, *wave_sems, side)
            advance(index)

            @pl.when(turn < FWD - 1)
            def _():
                value = wave[1 - slot, pl.ds(inside + chunk * index, chunk)]
                halo_start(value, *wave_halo, 1 - slot, *wave_sems, side)

        for index in range(1, chunks - 1):
            advance(index)

        for late in range(2):

            @pl.when(turn == FWD - 3 + late)
            def _():
                for index in range(chunks):
                    part = pl.ds(chunk * index, chunk)
                    term = (
                        wave[1 - slot, pl.ds(inside + chunk * index, chunk)]
                        * adj[ADJ - late, part]
                    )
                    image[part] = term if late == 0 else image[part] + term

        return carry

    lax.fori_loop(0, FWD, forward_step, 0)
    for index in range(chunks):
        part = pl.ds(chunk * index, chunk)
        image[part] = image[part] + wave[FWD % 2, pl.ds(inside + chunk * index, chunk)] * adj[1, part]

    theirs = (1 - core) * half
    mine = core * half
    swap = pltpu.make_async_remote_copy(
        src_ref=image.at[pl.ds(theirs, half)],
        dst_ref=from_core,
        send_sem=core_sem.at[0],
        recv_sem=core_sem.at[1],
        device_id=peer(partner),
        device_id_type=MESH,
    )
    swap.start()
    swap.wait()
    rows = size_y // chips
    for target in range(chips):
        cut = slice(target * rows, (target + 1) * rows)
        to_chip[target] = image[pl.ds(mine, half), cut] + from_core[:, cut]

    def chip_copy(target, landing):
        return pltpu.make_async_remote_copy(
            src_ref=to_chip.at[target],
            dst_ref=from_chip.at[landing],
            send_sem=chip_send.at[target],
            recv_sem=chip_recv.at[landing],
            device_id=peer(target * 2 + core),
            device_id_type=MESH,
        )

    def chip_start(turn, carry):
        chip_copy(lax.rem(chip + turn, chips), chip).start()
        return carry

    lax.fori_loop(1, chips, chip_start, 0)
    last[...] = to_chip[chip]

    def chip_add(turn, carry):
        other = lax.rem(chip + turn, chips)
        chip_copy(other, other).wait_recv()
        last[...] = last[...] + from_chip[other]
        return carry

    lax.fori_loop(1, chips, chip_add, 0)
    trade = pltpu.make_async_remote_copy(
        src_ref=last,
        dst_ref=last_in,
        send_sem=last_sem.at[0],
        recv_sem=last_sem.at[1],
        device_id=peer(partner),
        device_id_type=MESH,
    )
    trade.start()
    trade.wait()
    row_half = rows // 2
    first_core = core == 0
    for block, offset in ((last, mine), (last_in, theirs)):
        value = block[...]
        chosen = jnp.where(first_core, 1.0, 0.0)
        image_out[pl.ds(offset, half)] = (
            chosen * value[:, :row_half] + (1.0 - chosen) * value[:, row_half:]
        )

    def drain(turn, carry):
        other = lax.rem(me + turn, shots)
        for level in (1, 0):
            fetch_copy(level, other).wait_send()
        return carry

    lax.fori_loop(1, shots, drain, 0)

    def chip_drain(turn, carry):
        target = lax.rem(chip + turn, chips)
        chip_copy(target, chip).wait_send()
        return carry

    lax.fori_loop(1, chips, chip_drain, 0)
    result.wait()


def local(
    shots,
    spaces,
    courant,
    snapshot_store,
    slab_holder,
    snap_step,
    window_end,
    source_cell,
    wavelet,
    receiver_cells,
    residual_data,
    adjoint_prev,
    adjoint_now,
):
    planes, size_y, size_z = courant.shape
    slabs = snapshot_store.shape[0]
    cap = CAP
    chips = shots // 2
    rows = size_y // chips
    smem = pl.BlockSpec(memory_space=pltpu.SMEM)
    vmem = pl.BlockSpec(memory_space=pltpu.VMEM)
    anywhere = pl.BlockSpec(memory_space=pltpu.HBM)
    half = planes // 2
    padded = (2, planes + 2 * HALO, size_y, size_z)
    coded = (2, 2, HALO * size_y + SCALE_ROWS, size_z)
    dma = pltpu.SemaphoreType.DMA
    image, adjoint = pl.pallas_call(
        functools.partial(kernel, shots, spaces, cap),
        out_shape=(
            jax.ShapeDtypeStruct((planes, rows // 2, size_z), F32),
            jax.ShapeDtypeStruct((planes, size_y, size_z), F32),
        ),
        in_specs=[smem] * 5 + [vmem] * 2 + [anywhere] * 4,
        out_specs=(vmem, anywhere),
        scratch_shapes=[
            pltpu.VMEM((planes, size_y, size_z), F32),
            pltpu.VMEM((slabs, 2, size_y, size_z), BF16),
            pltpu.VMEM((ADJ + 2, planes, size_y, size_z), F32),
            pltpu.VMEM(padded, F32),
            pltpu.VMEM(padded, F32),
            pltpu.VMEM(coded, jnp.int16),
            pltpu.VMEM(coded, jnp.int16),
            pltpu.VMEM(coded, jnp.int16),
            pltpu.VMEM(coded, jnp.int16),
            pltpu.VMEM((2, shots * cap, size_y, size_z), BF16),
            pltpu.VMEM((2, shots * cap, size_y, size_z), BF16),
            pltpu.VMEM((size_z, size_z), BF16),
            pltpu.VMEM((HALO * size_y, HALO * size_y), BF16),
            pltpu.VMEM((size_y, size_z), F32),
            pltpu.VMEM((size_z, receiver_cells.shape[1]), BF16),
            pltpu.VMEM((planes, size_y, size_z), F32),
            pltpu.VMEM((half, size_y, size_z), F32),
            pltpu.VMEM((chips, half, rows, size_z), F32),
            pltpu.VMEM((chips, half, rows, size_z), F32),
            pltpu.VMEM((half, rows, size_z), F32),
            pltpu.VMEM((half, rows, size_z), F32),
            dma((4,)),
            dma((2, shots)),
            dma((2, shots)),
            dma((2, 2)),
            dma((2, 2)),
            dma((2, 2)),
            dma((2, 2)),
            dma((2,)),
            dma((chips,)),
            dma((chips,)),
            dma((2,)),
            dma((1,)),
        ],
        compiler_params=pltpu.CompilerParams(
            collective_id=0, has_side_effects=True, vmem_limit_bytes=48 * 2**20
        ),
    )(
        slab_holder,
        snap_step,
        window_end,
        source_cell,
        wavelet,
        receiver_cells,
        residual_data[0],
        courant,
        snapshot_store.reshape(slabs, 2, size_y, size_z),
        adjoint_prev[0],
        adjoint_now[0],
    )
    return (image * (1.0 / ADJ)).reshape(planes, rows // 2 * size_z), adjoint[None]


def solution(mesh):
    in_specs = (
        P("space", None, None),
        P("shot", None, "space", None, None),
        P(),
        P("shot"),
        P("shot"),
        P("shot"),
        P(),
        P("shot", None),
        P("shot", None, None),
        P("shot", "space", None, None),
        P("shot", "space", None, None),
    )
    out_specs = (P("space", "shot"), P("shot", "space", None, None))
    return jax.shard_map(
        functools.partial(local, mesh.shape["shot"], mesh.shape["space"]),
        mesh=mesh,
        in_specs=in_specs,
        out_specs=out_specs,
        check_vma=False,
    )
```

profile of v0, /device:TPU:57, one launch (start us, length us, event | category | flops | bytes accessed | tf_op | source)
XLA Modules:
  0.0 122.2 jit_solution(5685086763151823493)
XLA Ops:
  1.3 0.0 copy-start.7
  1.9 0.0 copy-start.4
  2.6 0.0 copy-done.7
  2.6 0.0 copy-start.5
  2.6 0.0 copy-start.6
  2.7 0.0 copy-done.4
  2.7 0.6 copy-done.5
  3.3 0.0 copy-done.6
  3.3 0.0 copy-start
  3.3 1.2 %copy-done = f32[16,64,256]{2,1,0:T(8,128)S(1)} copy-done((f32[16,64,256]{2,1,0:T(8,128)S(1)}, f32[16,64,256]{2,1,0:T(8,128)}, u32[]{:S(2)}) %copy-start) | copy-done | bytes 1048600
  4.5 0.0 copy-start.1
  4.5 1.2 %copy-done.1 = bf16[16,2,1,64,256]{4,3,2,1,0:T(8,128)(2,1)S(1)} copy-done((bf16[16,2,1,64,256]{4,3,2,1,0:T(8,128)(2,1)S(1)}, bf16[16,2,1,64,256]{4,3,2,1,0:T(8,128)(2,1)}, u32[]{:S(2)}) %copy-start.1) | copy-done | bytes 1048600
  5.8 0.0 copy-start.2
  5.8 1.2 %copy-done.2 = f32[1,16,64,256]{3,2,1,0:T(8,128)S(1)} copy-done((f32[1,16,64,256]{3,2,1,0:T(8,128)S(1)}, f32[1,16,64,256]{3,2,1,0:T(8,128)}, u32[]{:S(2)}) %copy-start.2) | copy-done | bytes 1048600
  7.0 0.0 copy-start.3
  7.0 1.2 %copy-done.3 = f32[1,16,64,256]{3,2,1,0:T(8,128)S(1)} copy-done((f32[1,16,64,256]{3,2,1,0:T(8,128)S(1)}, f32[1,16,64,256]{3,2,1,0:T(8,128)}, u32[]{:S(2)}) %copy-start.3) | copy-done | bytes 1048600
  8.2 112.3 %shard_map.122 = (f32[16,4,256]{2,1,0:T(4,128)S(1)}, f32[16,64,256]{2,1,0:T(8,128)S(1)}) custom-call(s32[16,16]{1,0:T(8,128)S(1)} %copy-done.4, s32[1]{0:T(128)S(6)} %copy.18.snap_step, s32[1]{0:T(128)S(6)} %copy.19.window_end, s32[1]{0:T(128)S(6)} %copy.20.source_cell, f32[64]{0:T(128)S(1)} %copy-done.6, s32[1,256]{1,0:T(1,128)S(1)} %copy-done.5, ...), custom_call_target="tpu_custom_call" | custom-call | tf_op jit(solution)/shard_map/pallas_call | solution.py:544
  120.6 0.6 copy.14
  121.2 1.0 copy.21
  (2 shorter events, 0.0 us)
Async XLA Ops:
  1.3 1.3 %copy-start.7 = (f32[1,3,256]{2,0,1:T(1,128)S(1)}, f32[1,3,256]{2,0,1:T(1,128)}, u32[]{:S(2)}) copy-start(f32[1,3,256]{2,0,1:T(1,128)} %param.19) | copy-start | bytes 9220
  1.9 0.7 copy-start.4
  2.6 0.7 copy-start.5
  2.6 0.7 copy-start.6
  3.3 1.2 %copy-start = (f32[16,64,256]{2,1,0:T(8,128)S(1)}, f32[16,64,256]{2,1,0:T(8,128)}, u32[]{:S(2)}) copy-start(f32[16,64,256]{2,1,0:T(8,128)} %courant_in.1) | copy-start | bytes 3145732
  4.5 1.2 %copy-start.1 = (bf16[16,2,1,64,256]{4,3,2,1,0:T(8,128)(2,1)S(1)}, bf16[16,2,1,64,256]{4,3,2,1,0:T(8,128)(2,1)}, u32[]{:S(2)}) copy-start(bf16[16,2,1,64,256]{4,3,2,1,0:T(8,128)(2,1)} %param.12) | copy-start | bytes 3145732
  5.8 1.2 %copy-start.2 = (f32[1,16,64,256]{3,2,1,0:T(8,128)S(1)}, f32[1,16,64,256]{3,2,1,0:T(8,128)}, u32[]{:S(2)}) copy-start(f32[1,16,64,256]{3,2,1,0:T(8,128)} %param.20) | copy-start | bytes 3145732
  7.0 1.2 %copy-start.3 = (f32[1,16,64,256]{3,2,1,0:T(8,128)S(1)}, f32[1,16,64,256]{3,2,1,0:T(8,128)}, u32[]{:S(2)}) copy-start(f32[1,16,64,256]{3,2,1,0:T(8,128)} %param.21) | copy-start | bytes 3145732
where the time goes:
time: 123 us; the launch traced here: 122 us
  Pallas kernels  112 us (91%)
  local copies, waits for them, and re-layouts  7.18 us (6%)
  between operations  2.67 us (2%)
    pallas_call x1, Pallas kernels, local(): pl.pallas_call(functools.partial(kernel, shots, spaces, cap), out_shape=(...  112 us
    unnamed x19, local copies, waits for them, and re-layouts  7.18 us

commit v1 on v0

v1 whole, which is shorter than its diff:
```python
import functools

import jax
import jax.numpy as jnp
from jax import lax
from jax.experimental import pallas as pl
from jax.experimental.pallas import tpu as pltpu
from jax.sharding import PartitionSpec as P

FWD = 8
ADJ = 3
HALO = 4
CAP = 2
SCALE = 5040.0
TAPS = (8064.0, -1008.0, 128.0, -9.0)
CENTRE_Z = -43008.0
CENTRE_Y = -42.0
CODE_BITS = 13.0
SCALE_ROWS = 16
MESH = pl.DeviceIdType.MESH
F32 = jnp.float32
BF16 = jnp.bfloat16


def band(size, block, centre):
    row = lax.broadcasted_iota(jnp.int32, (size, size), 0)
    col = lax.broadcasted_iota(jnp.int32, (size, size), 1)
    gap = jnp.abs(row - col)
    result = jnp.where(gap == 0, centre, 0.0)
    for offset, tap in enumerate(TAPS, 1):
        result = jnp.where(gap == offset, tap, result)
    if block < size:
        result = jnp.where(row // block == col // block, result, 0.0)
    return result.astype(BF16)


def split(value):
    high = value.astype(BF16)
    return high, (value - high.astype(F32)).astype(BF16)


def encode(value):
    rows = value.shape[0] * value.shape[1]
    flat = value.reshape(rows, value.shape[2])
    top = jnp.max(jnp.abs(flat), axis=0, keepdims=True)
    power = jnp.floor(jnp.log2(jnp.maximum(top, 1e-30)))
    code = jnp.round(flat * jnp.exp2(CODE_BITS - power)).astype(jnp.int32).astype(jnp.int16)
    scale = jnp.broadcast_to(power.astype(jnp.int32), (SCALE_ROWS, value.shape[2])).astype(jnp.int16)
    return code, scale


def decode(code, scale, shape):
    power = scale.astype(jnp.int32).astype(F32)[:1]
    return (code.astype(jnp.int32).astype(F32) * jnp.exp2(power - CODE_BITS)).reshape(shape)


def kernel(
    shots,
    spaces,
    cap,
    holder,
    snap_step,
    window_end,
    source_cell,
    wavelet,
    cells,
    residual,
    courant_in,
    store_in,
    prev_in,
    now_in,
    image_out,
    adjoint_out,
    courant,
    store,
    adj,
    field,
    wave,
    adj_code,
    adj_land,
    wave_code,
    wave_land,
    packed,
    landed_old,
    landed_new,
    band_z,
    band_y,
    spot,
    col_hot,
    image,
    split_image,
    from_core,
    to_chip,
    from_chip,
    sent_slots,
    own_slots,
    local_sem,
    fetch_send,
    fetch_recv,
    courant_send,
    courant_recv,
    adj_send,
    adj_recv,
    wave_send,
    wave_recv,
    core_send,
    core_recv,
    chip_send,
    chip_recv,
    out_sem,
):
    me = lax.axis_index("shot")
    place = lax.axis_index("space")
    slabs, _, size_y, size_z = store.shape
    planes = courant.shape[0] - 2 * HALO
    has_low = place > 0
    has_high = place < spaces - 1
    has_side = (has_low, has_high)
    core = lax.rem(me, 2)
    chip = lax.div(me, 2)
    chips = shots // 2
    partner = chip * 2 + 1 - core
    chunk = HALO
    chunks = planes // chunk
    deep = 2 * HALO
    edges = (0, chunks - 1)
    inner = tuple(range(1, chunks - 1))

    landed = (landed_old, landed_new)

    def peer(shot):
        return (shot, place)

    own_planes = pl.ds(HALO, planes)
    loads = [
        pltpu.make_async_copy(now_in, adj.at[1], local_sem.at[0]),
        pltpu.make_async_copy(courant_in, courant.at[own_planes], local_sem.at[1]),
        pltpu.make_async_copy(store_in, store, local_sem.at[2]),
        pltpu.make_async_copy(prev_in, adj.at[0], local_sem.at[3]),
    ]
    for load in loads:
        load.start()

    barrier = pltpu.get_barrier_semaphore()

    def greet(turn, carry):
        other = lax.rem(me + turn, shots)
        pl.semaphore_signal(barrier, inc=1, device_id=peer(other), device_id_type=MESH)
        return carry

    for side in range(2):

        @pl.when(has_side[side])
        def _():
            pl.semaphore_signal(
                barrier, inc=1, device_id=(me, place + 2 * side - 1), device_id_type=MESH
            )

    lax.fori_loop(1, shots, greet, 0)

    def find_sent(other, carry):
        found = jnp.int32(0)
        spots = [jnp.int32(0)] * cap
        for slab in range(slabs):
            slot = holder[other, slab]
            mine = lax.div(slot, slabs) == me
            where = lax.rem(slot, slabs)
            for rank in range(cap):
                spots[rank] = jnp.where(jnp.logical_and(mine, found == rank), where, spots[rank])
            found = found + jnp.where(mine, 1, 0)
        for rank in range(cap):
            sent_slots[other * cap + rank] = spots[rank]
        return carry

    lax.fori_loop(0, shots, find_sent, 0)

    def find_own(slab, carry):
        storer = lax.div(holder[me, slab], slabs)
        rank = jnp.int32(0)
        for before in range(slabs):
            same = jnp.logical_and(lax.div(holder[me, before], slabs) == storer, before < slab)
            rank = rank + jnp.where(same, 1, 0)
        own_slots[slab] = storer * cap + rank
        return carry

    band_z[...] = band(size_z, size_z, CENTRE_Z)
    band_y[...] = band(chunk * size_y, size_y, CENTRE_Y)
    for side in range(2):

        @pl.when(jnp.logical_not(has_side[side]))
        def _():
            nothing = jnp.zeros((HALO, size_y, size_z), F32)
            courant[pl.ds((planes + HALO) * side, HALO)] = nothing
            for slot in range(2):
                field[slot, pl.ds((planes + HALO) * side, HALO)] = nothing
                for piece in range(2):
                    wave[slot, pl.ds((planes + deep) * side + HALO * piece, HALO)] = nothing

    halo_rows = HALO * size_y
    edge_shape = (HALO, size_y, size_z)

    def adj_copy(slot, side):
        return pltpu.make_async_remote_copy(
            src_ref=adj_code.at[slot, side],
            dst_ref=adj_land.at[slot, side],
            send_sem=adj_send.at[slot, side],
            recv_sem=adj_recv.at[slot, side],
            device_id=(me, place + 2 * side - 1),
            device_id_type=MESH,
        )

    def adj_start(value, slot, side):
        @pl.when(has_side[side])
        def _():
            numbers, scale = encode(value)
            adj_code[slot, side, :halo_rows] = numbers
            adj_code[slot, side, halo_rows:] = scale
            adj_copy(slot, side).start()

    def adj_wait(slot, side):
        @pl.when(has_side[side])
        def _():
            adj_copy(slot, side).wait_send()
            adj_copy(slot, 1 - side).wait_recv()
            field[slot, pl.ds((HALO + planes) * side, HALO)] = decode(
                adj_land[slot, 1 - side, :halo_rows], adj_land[slot, 1 - side, halo_rows:], edge_shape
            )

    def wave_copy(slot, side, piece):
        return pltpu.make_async_remote_copy(
            src_ref=wave_code.at[slot, side, piece],
            dst_ref=wave_land.at[slot, side, piece],
            send_sem=wave_send.at[slot, side, piece],
            recv_sem=wave_recv.at[slot, side, piece],
            device_id=(me, place + 2 * side - 1),
            device_id_type=MESH,
        )

    def wave_start(level, slot, side, piece):
        index = piece if side == 0 else chunks - 1 - piece

        @pl.when(has_side[side])
        def _():
            numbers, scale = encode(wave[level, pl.ds(deep + chunk * index, chunk)])
            wave_code[slot, side, piece, :halo_rows] = numbers
            wave_code[slot, side, piece, halo_rows:] = scale
            wave_copy(slot, side, piece).start()

    def wave_wait(level, slot, side, piece):
        index = -1 - piece if side == 0 else chunks + piece

        @pl.when(has_side[side])
        def _():
            wave_copy(slot, side, piece).wait_send()
            wave_copy(slot, 1 - side, piece).wait_recv()
            wave[level, pl.ds(deep + chunk * index, chunk)] = decode(
                wave_land[slot, 1 - side, piece, :halo_rows],
                wave_land[slot, 1 - side, piece, halo_rows:],
                edge_shape,
            )

    def courant_copy(side):
        return pltpu.make_async_remote_copy(
            src_ref=courant_in.at[pl.ds((planes - HALO) * side, HALO)],
            dst_ref=courant.at[pl.ds((planes + HALO) * (1 - side), HALO)],
            send_sem=courant_send.at[side],
            recv_sem=courant_recv.at[side],
            device_id=(me, place + 2 * side - 1),
            device_id_type=MESH,
        )

    def stencil(ref, slot, first):
        middle = ref[slot, pl.ds(first, chunk)]
        high, low = split(middle.reshape(chunk * size_y, size_z))
        right = band_z[...]
        left = band_y[...]
        total = jnp.dot(high, right, preferred_element_type=F32)
        total += jnp.dot(low, right, preferred_element_type=F32)
        total += jnp.dot(left, high, preferred_element_type=F32)
        total += jnp.dot(left, low, preferred_element_type=F32)
        total = total.reshape(chunk, size_y, size_z)
        for offset, tap in enumerate(TAPS, 1):
            total += tap * (
                ref[slot, pl.ds(first + offset, chunk)] + ref[slot, pl.ds(first - offset, chunk)]
            )
        return total

    def first_field(index):
        part = pl.ds(HALO + chunk * index, chunk)
        scaled = courant[part] * (1.0 / SCALE)
        courant[part] = scaled
        value = scaled * adj[1, pl.ds(chunk * index, chunk)]
        field[0, part] = value
        return value

    loads[0].wait()
    loads[1].wait()
    low_count = jnp.where(has_low, 1, 0)
    high_count = jnp.where(has_high, 1, 0)
    pl.semaphore_wait(barrier, shots - 1 + low_count + high_count)
    for side, index in enumerate(edges):
        adj_start(first_field(index), 0, side)

    def fetch_copy(level, other):
        return pltpu.make_async_remote_copy(
            src_ref=packed.at[level, pl.ds(other * cap, cap)],
            dst_ref=landed[level].at[pl.ds(me * cap, cap)],
            send_sem=fetch_send.at[level, other],
            recv_sem=fetch_recv.at[level, me],
            device_id=peer(other),
            device_id_type=MESH,
        )

    def fetch_arrival(level, other):
        return pltpu.make_async_remote_copy(
            src_ref=packed.at[level, pl.ds(other * cap, cap)],
            dst_ref=landed[level].at[pl.ds(other * cap, cap)],
            send_sem=fetch_send.at[level, other],
            recv_sem=fetch_recv.at[level, other],
            device_id=peer(other),
            device_id_type=MESH,
        )

    loads[2].wait()
    for level in (1, 0):

        def pack(turn, carry):
            other = lax.rem(me + turn, shots)
            for rank in range(cap):
                packed[level, other * cap + rank] = store[sent_slots[other * cap + rank], level]
            fetch_copy(level, other).start()
            return carry

        lax.fori_loop(1, shots, pack, 0)

    for rank in range(cap):
        for level in (1, 0):
            landed[level][me * cap + rank] = store[sent_slots[me * cap + rank], level]

    for side in range(2):

        @pl.when(has_side[side])
        def _():
            courant_copy(side).start()

    for index in inner:
        first_field(index)
    lax.fori_loop(0, slabs, find_own, 0)

    plane_cells = size_y * size_z
    source = source_cell[0]
    source_plane = lax.div(source, plane_cells) - place * planes
    in_plane = lax.rem(source, plane_cells)
    flat = lax.broadcasted_iota(jnp.int32, (size_y, size_z), 0) * size_z + lax.broadcasted_iota(
        jnp.int32, (size_y, size_z), 1
    )
    spot[...] = jnp.where(flat == in_plane, 1.0, 0.0)

    recv_cells = cells[...]
    recv_row = recv_cells // size_z - place * (planes * size_y)
    recv_col = recv_cells % size_z
    count = recv_cells.shape[1]
    col_hot[...] = jnp.where(
        lax.broadcasted_iota(jnp.int32, (size_z, count), 0) == recv_col, 1.0, 0.0
    ).astype(BF16)

    loads[3].wait()

    def adjoint_step(turn, carry):
        slot = lax.rem(turn, 2)
        data = residual[0, pl.ds(turn, 1)]
        data_high, data_low = split(data)
        data_high = data_high.astype(F32)
        data_low = data_low.astype(F32)
        hot = col_hot[...]

        def advance(index):
            part = pl.ds(chunk * index, chunk)
            padded = pl.ds(HALO + chunk * index, chunk)
            row = lax.broadcasted_iota(jnp.int32, (chunk * size_y, count), 0) + (
                chunk * size_y * index
            )
            hit = row == recv_row
            total = lax.dot_general(
                jnp.where(hit, data_high, 0.0).astype(BF16),
                hot,
                (((1,), (1,)), ((), ())),
                preferred_element_type=F32,
            )
            total += lax.dot_general(
                jnp.where(hit, data_low, 0.0).astype(BF16),
                hot,
                (((1,), (1,)), ((), ())),
                preferred_element_type=F32,
            )
            total = total.reshape(chunk, size_y, size_z) + stencil(
                field, slot, HALO + chunk * index
            )
            current = adj[turn + 1, part]
            following = (current + current) - adj[turn, part] + total
            adj[turn + 2, part] = following
            field[1 - slot, padded] = courant[padded] * following

        for side, index in enumerate(edges):
            adj_wait(slot, side)
            advance(index)

            @pl.when(turn < ADJ - 1)
            def _():
                adj_start(field[1 - slot, pl.ds(HALO + chunk * index, chunk)], 1 - slot, side)

        for index in inner:
            advance(index)
        return carry

    lax.fori_loop(0, ADJ - 1, adjoint_step, 0)

    def arrive(level):
        def one(turn, carry):
            fetch_arrival(level, lax.rem(me + turn, shots)).wait_recv()
            return carry

        lax.fori_loop(1, shots, one, 0)

    arrive(1)

    def unpack(slab, carry):
        wave[0, deep + slab] = landed_new[own_slots[slab]].astype(F32)
        return carry

    lax.fori_loop(0, slabs, unpack, 0)
    for side in range(2):
        wave_start(0, 0, side, 0)

    steps = window_end[0] - snap_step[0]
    start = snap_step[0]

    def image_term(level, turn, index):
        behind = steps - turn
        weight = jnp.where(jnp.logical_and(behind >= 0, behind < ADJ), 1.0, 0.0)
        state = adj[1 + jnp.clip(behind, 0, ADJ - 1), pl.ds(chunk * index, chunk)]
        return (weight * state) * wave[level, pl.ds(deep + chunk * index, chunk)]

    def image_add(level, turn):
        for index in range(chunks):
            part = pl.ds(chunk * index, chunk)
            image[part] = image[part] + image_term(level, turn, index)

    def advance(level, turn, index, older=True):
        first = deep + chunk * index
        here = pl.ds(first, chunk)
        middle = wave[level, here]
        total = courant[pl.ds(first - HALO, chunk)] * stencil(wave, level, first)
        total = total + (middle + middle)
        if older:
            total = total - wave[1 - level, here]
        amplitude = wavelet[start + turn]
        pattern = spot[...]
        for plane in range(chunk):
            push = jnp.where(source_plane == chunk * index + plane, amplitude, 0.0)
            wave[1 - level, first + plane] = total[plane] + push * pattern

    for index in inner:
        advance(0, 0, index, older=False)
    for index in range(chunks):
        image[pl.ds(chunk * index, chunk)] = image_term(0, 0, index)
    adjoint_step(ADJ - 1, 0)
    result = pltpu.make_async_copy(adj.at[ADJ + 1], adjoint_out, out_sem.at[0])
    result.start()
    for side, index in enumerate(edges):
        wave_wait(0, 0, side, 0)
        advance(0, 0, index, older=False)
    arrive(0)

    def less(slab, carry):
        here = deep + slab
        wave[1, here] = wave[1, here] - landed_old[own_slots[slab]].astype(F32)
        return carry

    half = planes // 2
    for side in range(2):
        lax.fori_loop(half * side, half * (side + 1), less, 0)
        for piece in range(2):
            wave_start(1, 1, side, piece)

    for side in range(2):

        @pl.when(has_side[side])
        def _():
            courant_copy(side).wait_send()
            courant_copy(1 - side).wait_recv()
            part = pl.ds((planes + HALO) * side, HALO)
            courant[part] = courant[part] * (1.0 / SCALE)

    blocks = (FWD - 2) // 2

    def block(number, carry):
        turn = 1 + 2 * number
        slot = lax.rem(number + 1, 2)
        for index in inner:
            advance(1, turn, index)
        image_add(1, turn)
        for side in range(2):
            order = (0, 1) if side == 0 else (chunks - 1, chunks - 2)
            outside = -1 if side == 0 else chunks
            wave_wait(1, slot, side, 0)
            advance(1, turn, order[0])
            wave_wait(1, slot, side, 1)
            advance(1, turn, outside)
            advance(0, turn + 1, order[0])
            wave_start(1, 1 - slot, side, 0)
            advance(0, turn + 1, order[1])

            @pl.when(number < blocks - 1)
            def _():
                wave_start(1, 1 - slot, side, 1)

        image_add(0, turn + 1)
        return carry

    lax.fori_loop(0, blocks, block, 0)

    rows = size_y // chips
    row_half = rows // 2

    def cut_image(piece, place_in, index):
        value = image[pl.ds(chunk * index, chunk)] + image_term(0, FWD, index)
        for target in range(chips):
            for side in range(2):
                low = target * rows + side * row_half
                split_image[side, piece, target, pl.ds(chunk * place_in, chunk)] = value[
                    :, low : low + row_half
                ]

    def core_copy(piece):
        return pltpu.make_async_remote_copy(
            src_ref=split_image.at[1 - core, piece],
            dst_ref=from_core.at[piece],
            send_sem=core_send.at[piece],
            recv_sem=core_recv.at[piece],
            device_id=peer(partner),
            device_id_type=MESH,
        )

    def chip_copy(piece, target, landing):
        return pltpu.make_async_remote_copy(
            src_ref=to_chip.at[piece, target],
            dst_ref=from_chip.at[piece, landing],
            send_sem=chip_send.at[piece, target],
            recv_sem=chip_recv.at[piece, landing],
            device_id=peer(target * 2 + core),
            device_id_type=MESH,
        )

    def to_chips(piece):
        core_copy(piece).wait()

        def one(turn, carry):
            target = lax.rem(chip + turn, chips)
            to_chip[piece, target] = split_image[core, piece, target] + from_core[piece, target]
            chip_copy(piece, target, chip).start()
            return carry

        lax.fori_loop(1, chips, one, 0)
        to_chip[piece, chip] = split_image[core, piece, chip] + from_core[piece, chip]

    for index in inner:
        advance(1, FWD - 1, index)
    for order, index in enumerate(inner):
        image[pl.ds(chunk * index, chunk)] = image[pl.ds(chunk * index, chunk)] + image_term(
            1, FWD - 1, index
        )
        cut_image(0, order, index)
    core_copy(0).start()
    for index in edges:
        image[pl.ds(chunk * index, chunk)] = image[pl.ds(chunk * index, chunk)] + image_term(
            1, FWD - 1, index
        )
    to_chips(0)
    last_slot = (blocks + 1) % 2
    for side, index in enumerate(edges):
        wave_wait(1, last_slot, side, 0)
        advance(1, FWD - 1, index)
        cut_image(1, side, index)
    core_copy(1).start()
    to_chips(1)

    for piece in range(2):

        def add(turn, carry):
            other = lax.rem(chip + turn, chips)
            chip_copy(piece, other, other).wait_recv()
            chip_copy(piece, other, chip).wait_send()
            to_chip[piece, chip] = to_chip[piece, chip] + from_chip[piece, other]
            return carry

        lax.fori_loop(1, chips, add, 0)
        total = to_chip[piece, chip]
        for order, index in enumerate((inner, edges)[piece]):
            image_out[pl.ds(chunk * index, chunk)] = total[chunk * order : chunk * (order + 1)]

    def drain(turn, carry):
        other = lax.rem(me + turn, shots)
        for level in (1, 0):
            fetch_copy(level, other).wait_send()
        return carry

    lax.fori_loop(1, shots, drain, 0)
    result.wait()


def local(
    shots,
    spaces,
    courant,
    snapshot_store,
    slab_holder,
    snap_step,
    window_end,
    source_cell,
    wavelet,
    receiver_cells,
    residual_data,
    adjoint_prev,
    adjoint_now,
):
    planes, size_y, size_z = courant.shape
    slabs = snapshot_store.shape[0]
    cap = CAP
    chips = shots // 2
    rows = size_y // chips
    smem = pl.BlockSpec(memory_space=pltpu.SMEM)
    vmem = pl.BlockSpec(memory_space=pltpu.VMEM)
    hbm = pl.BlockSpec(memory_space=pltpu.HBM)
    half = planes // 2
    coded = (HALO * size_y + SCALE_ROWS, size_z)
    dma = pltpu.SemaphoreType.DMA
    image, adjoint = pl.pallas_call(
        functools.partial(kernel, shots, spaces, cap),
        out_shape=(
            jax.ShapeDtypeStruct((planes, rows // 2, size_z), F32),
            jax.ShapeDtypeStruct((planes, size_y, size_z), F32),
        ),
        in_specs=[smem] * 5 + [vmem] * 2 + [hbm] * 4,
        out_specs=(vmem, hbm),
        scratch_shapes=[
            pltpu.VMEM((planes + 2 * HALO, size_y, size_z), F32),
            pltpu.VMEM((slabs, 2, size_y, size_z), BF16),
            pltpu.VMEM((ADJ + 2, planes, size_y, size_z), F32),
            pltpu.VMEM((2, planes + 2 * HALO, size_y, size_z), F32),
            pltpu.VMEM((2, planes + 4 * HALO, size_y, size_z), F32),
            pltpu.VMEM((2, 2) + coded, jnp.int16),
            pltpu.VMEM((2, 2) + coded, jnp.int16),
            pltpu.VMEM((2, 2, 2) + coded, jnp.int16),
            pltpu.VMEM((2, 2, 2) + coded, jnp.int16),
            pltpu.VMEM((2, shots * cap, size_y, size_z), BF16),
            pltpu.VMEM((shots * cap, size_y, size_z), BF16),
            pltpu.VMEM((shots * cap, size_y, size_z), BF16),
            pltpu.VMEM((size_z, size_z), BF16),
            pltpu.VMEM((HALO * size_y, HALO * size_y), BF16),
            pltpu.VMEM((size_y, size_z), F32),
            pltpu.VMEM((size_z, receiver_cells.shape[1]), BF16),
            pltpu.VMEM((planes, size_y, size_z), F32),
            pltpu.VMEM((2, 2, chips, half, rows // 2, size_z), F32),
            pltpu.VMEM((2, chips, half, rows // 2, size_z), F32),
            pltpu.VMEM((2, chips, half, rows // 2, size_z), F32),
            pltpu.VMEM((2, chips, half, rows // 2, size_z), F32),
            pltpu.SMEM((shots * cap,), jnp.int32),
            pltpu.SMEM((slabs,), jnp.int32),
            dma((4,)),
            dma((2, shots)),
            dma((2, shots)),
            dma((2,)),
            dma((2,)),
            dma((2, 2)),
            dma((2, 2)),
            dma((2, 2, 2)),
            dma((2, 2, 2)),
            dma((2,)),
            dma((2,)),
            dma((2, chips)),
            dma((2, chips)),
            dma((1,)),
        ],
        compiler_params=pltpu.CompilerParams(
            collective_id=0, has_side_effects=True, vmem_limit_bytes=63 * 2**20
        ),
    )(
        slab_holder,
        snap_step,
        window_end,
        source_cell,
        wavelet,
        receiver_cells,
        residual_data,
        courant,
        snapshot_store.reshape(slabs, 2, size_y, size_z),
        adjoint_prev[0],
        adjoint_now[0],
    )
    return (image * (1.0 / ADJ)).reshape(planes, rows // 2 * size_z), adjoint[None]


def solution(mesh):
    in_specs = (
        P("space", None, None),
        P("shot", None, "space", None, None),
        P(),
        P("shot"),
        P("shot"),
        P("shot"),
        P(),
        P("shot", None),
        P("shot", None, None),
        P("shot", "space", None, None),
        P("shot", "space", None, None),
    )
    out_specs = (P("space", "shot"), P("shot", "space", None, None))
    return jax.shard_map(
        functools.partial(local, mesh.shape["shot"], mesh.shape["space"]),
        mesh=mesh,
        in_specs=in_specs,
        out_specs=out_specs,
        check_vma=False,
    )
```

time: 123 us -> 109 us (0.89)
  the two profiles are of different devices: /device:TPU:57 before, /device:TPU:248 now
where the time goes in v1:
time: 109 us
  Pallas kernels  101 us (93%)
  local copies, waits for them, and re-layouts  4.21 us (4%)
  between operations  2.59 us (2%)
    pallas_call x1, Pallas kernels, local(): pl.pallas_call(functools.partial(kernel, shots, spaces, cap), out_shape=(...  101 us
    unnamed x5, local copies, waits for them, and re-layouts  4.21 us

profile of v1, /device:TPU:248, one launch (start us, length us, event | category | flops | bytes accessed | tf_op | source)
XLA Modules:
  0.0 108.6 jit_solution(7207372101813463)
XLA Ops:
  2.6 0.0 copy-start
  2.6 0.7 copy-done
  3.3 0.6 copy.13.residual
  3.8 100.9 %shard_map.122 = (f32[16,4,256]{2,1,0:T(4,128)}, f32[16,64,256]{2,1,0:T(8,128)}) custom-call(s32[16,16]{1,0:T(8,128)} %holder.1, s32[1]{0:T(128)S(6)} %copy.16.snap_step, s32[1]{0:T(128)S(6)} %copy.17.window_end, s32[1]{0:T(128)S(6)} %copy.18.source_cell, f32[64]{0:T(128)} %wavelet.1, s32[1,256]{1,0:T(1,128)} %cells.1, f32[1,3,256]{2,1,0:T(4,128)} %copy.13.residual, ...), custom_call_target="tpu_custom_call" | custom-call | tf_op jit(solution)/shard_map/pallas_call | solution.py:638
  104.8 0.9 broadcast_multiply_fusion
  105.6 0.6 copy.14
  106.3 2.3 %copy.19 = f32[1,16,64,256]{3,2,1,0:T(8,128)} copy(f32[1,16,64,256]{3,2,1,0:T(8,128)} %bitcast.9) | data formatting | bytes 2097152
Async XLA Ops:
  2.6 0.7 copy-start

commit v2 on v1

--- a/solution.py
+++ b/solution.py
@@ -87,6 +87,7 @@
     band_y,
     spot,
     col_hot,
+    sums,
     image,
     split_image,
     from_core,
@@ -158,7 +159,7 @@
 
     lax.fori_loop(1, shots, greet, 0)
 
-    def find_sent(other, carry):
+    def find_sent(other):
         found = jnp.int32(0)
         spots = [jnp.int32(0)] * cap
         for slab in range(slabs):
@@ -170,9 +171,6 @@
             found = found + jnp.where(mine, 1, 0)
         for rank in range(cap):
             sent_slots[other * cap + rank] = spots[rank]
-        return carry
-
-    lax.fori_loop(0, shots, find_sent, 0)
 
     def find_own(slab, carry):
         storer = lax.div(holder[me, slab], slabs)
@@ -183,42 +181,48 @@
         own_slots[slab] = storer * cap + rank
         return carry
 
-    band_z[...] = band(size_z, size_z, CENTRE_Z)
-    band_y[...] = band(chunk * size_y, size_y, CENTRE_Y)
-    for side in range(2):
-
-        @pl.when(jnp.logical_not(has_side[side]))
-        def _():
-            nothing = jnp.zeros((HALO, size_y, size_z), F32)
-            courant[pl.ds((planes + HALO) * side, HALO)] = nothing
-            for slot in range(2):
-                field[slot, pl.ds((planes + HALO) * side, HALO)] = nothing
-                for piece in range(2):
-                    wave[slot, pl.ds((planes + deep) * side + HALO * piece, HALO)] = nothing
-
     halo_rows = HALO * size_y
     edge_shape = (HALO, size_y, size_z)
 
-    def adj_copy(slot, side):
+    def pick(turn, values):
+        result = jnp.int32(values[0])
+        for at, value in enumerate(values[1:], 1):
+            result = jnp.where(turn == at, value, result)
+        return result
+
+    def neighbour(side):
+        other = place + 2 * side - 1
+        return other, jnp.logical_and(other >= 0, other < spaces)
+
+    def remote(source, target, send, recv, side):
         return pltpu.make_async_remote_copy(
-            src_ref=adj_code.at[slot, side],
-            dst_ref=adj_land.at[slot, side],
-            send_sem=adj_send.at[slot, side],
-            recv_sem=adj_recv.at[slot, side],
+            src_ref=source,
+            dst_ref=target,
+            send_sem=send,
+            recv_sem=recv,
             device_id=(me, place + 2 * side - 1),
             device_id_type=MESH,
         )
 
-    def adj_start(value, slot, side):
-        @pl.when(has_side[side])
-        def _():
-            numbers, scale = encode(value)
+    def adj_copy(slot, side):
+        return remote(
+            adj_code.at[slot, side],
+            adj_land.at[slot, side],
+            adj_send.at[slot, side],
+            adj_recv.at[slot, side],
+            side,
+        )
+
+    def adj_start(index, slot, side):
+        @pl.when(neighbour(side)[1])
+        def _():
+            numbers, scale = encode(field[slot, pl.ds(HALO + chunk * index, chunk)])
             adj_code[slot, side, :halo_rows] = numbers
             adj_code[slot, side, halo_rows:] = scale
             adj_copy(slot, side).start()
 
     def adj_wait(slot, side):
-        @pl.when(has_side[side])
+        @pl.when(neighbour(side)[1])
         def _():
             adj_copy(slot, side).wait_send()
             adj_copy(slot, 1 - side).wait_recv()
@@ -227,19 +231,18 @@
             )
 
     def wave_copy(slot, side, piece):
-        return pltpu.make_async_remote_copy(
-            src_ref=wave_code.at[slot, side, piece],
-            dst_ref=wave_land.at[slot, side, piece],
-            send_sem=wave_send.at[slot, side, piece],
-            recv_sem=wave_recv.at[slot, side, piece],
-            device_id=(me, place + 2 * side - 1),
-            device_id_type=MESH,
+        return remote(
+            wave_code.at[slot, side, piece],
+            wave_land.at[slot, side, piece],
+            wave_send.at[slot, side, piece],
+            wave_recv.at[slot, side, piece],
+            side,
         )
 
     def wave_start(level, slot, side, piece):
-        index = piece if side == 0 else chunks - 1 - piece
-
-        @pl.when(has_side[side])
+        index = piece + side * (chunks - 1 - 2 * piece)
+
+        @pl.when(neighbour(side)[1])
         def _():
             numbers, scale = encode(wave[level, pl.ds(deep + chunk * index, chunk)])
             wave_code[slot, side, piece, :halo_rows] = numbers
@@ -247,9 +250,9 @@
             wave_copy(slot, side, piece).start()
 
     def wave_wait(level, slot, side, piece):
-        index = -1 - piece if side == 0 else chunks + piece
-
-        @pl.when(has_side[side])
+        index = -1 - piece + side * (chunks + 1 + 2 * piece)
+
+        @pl.when(neighbour(side)[1])
         def _():
             wave_copy(slot, side, piece).wait_send()
             wave_copy(slot, 1 - side, piece).wait_recv()
@@ -260,16 +263,15 @@
             )
 
     def courant_copy(side):
-        return pltpu.make_async_remote_copy(
-            src_ref=courant_in.at[pl.ds((planes - HALO) * side, HALO)],
-            dst_ref=courant.at[pl.ds((planes + HALO) * (1 - side), HALO)],
-            send_sem=courant_send.at[side],
-            recv_sem=courant_recv.at[side],
-            device_id=(me, place + 2 * side - 1),
-            device_id_type=MESH,
+        return remote(
+            courant_in.at[pl.ds((planes - HALO) * side, HALO)],
+            courant.at[pl.ds((planes + HALO) * (1 - side), HALO)],
+            courant_send.at[side],
+            courant_recv.at[side],
+            side,
         )
 
-    def stencil(ref, slot, first):
+    def flat_part(ref, slot, first):
         middle = ref[slot, pl.ds(first, chunk)]
         high, low = split(middle.reshape(chunk * size_y, size_z))
         right = band_z[...]
@@ -278,28 +280,36 @@
         total += jnp.dot(low, right, preferred_element_type=F32)
         total += jnp.dot(left, high, preferred_element_type=F32)
         total += jnp.dot(left, low, preferred_element_type=F32)
-        total = total.reshape(chunk, size_y, size_z)
+        return total
+
+    def deep_part(ref, slot, at, width):
+        total = None
         for offset, tap in enumerate(TAPS, 1):
-            total += tap * (
-                ref[slot, pl.ds(first + offset, chunk)] + ref[slot, pl.ds(first - offset, chunk)]
-            )
+            term = tap * (ref[slot, pl.ds(at + offset, width)] + ref[slot, pl.ds(at - offset, width)])
+            total = term if total is None else total + term
         return total
 
-    def first_field(index):
+    order = (0, chunks - 1) + inner
+
+    def first_field(turn, carry):
+        index = pick(turn, order)
         part = pl.ds(HALO + chunk * index, chunk)
         scaled = courant[part] * (1.0 / SCALE)
         courant[part] = scaled
-        value = scaled * adj[1, pl.ds(chunk * index, chunk)]
-        field[0, part] = value
-        return value
+        field[0, part] = scaled * adj[1, pl.ds(chunk * index, chunk)]
+
+        @pl.when(turn < 2)
+        def _():
+            adj_start(index, 0, turn)
+
+        return carry
 
     loads[0].wait()
     loads[1].wait()
     low_count = jnp.where(has_low, 1, 0)
     high_count = jnp.where(has_high, 1, 0)
     pl.semaphore_wait(barrier, shots - 1 + low_count + high_count)
-    for side, index in enumerate(edges):
-        adj_start(first_field(index), 0, side)
+    lax.fori_loop(0, chunks, first_field, 0)
 
     def fetch_copy(level, other):
         return pltpu.make_async_remote_copy(
@@ -326,16 +336,25 @@
 
         def pack(turn, carry):
             other = lax.rem(me + turn, shots)
+            if level == 1:
+                find_sent(other)
             for rank in range(cap):
                 packed[level, other * cap + rank] = store[sent_slots[other * cap + rank], level]
-            fetch_copy(level, other).start()
+
+            @pl.when(turn < shots)
+            def _():
+                fetch_copy(level, other).start()
+
             return carry
 
-        lax.fori_loop(1, shots, pack, 0)
-
-    for rank in range(cap):
+        lax.fori_loop(1, shots + 1, pack, 0)
+
+    def keep(rank, carry):
         for level in (1, 0):
-            landed[level][me * cap + rank] = store[sent_slots[me * cap + rank], level]
+            landed[level][me * cap + rank] = packed[level, me * cap + rank]
+        return carry
+
+    lax.fori_loop(0, cap, keep, 0)
 
     for side in range(2):
 
@@ -343,8 +362,19 @@
         def _():
             courant_copy(side).start()
 
-    for index in inner:
-        first_field(index)
+    band_z[...] = band(size_z, size_z, CENTRE_Z)
+    band_y[...] = band(chunk * size_y, size_y, CENTRE_Y)
+    for side in range(2):
+
+        @pl.when(jnp.logical_not(has_side[side]))
+        def _():
+            nothing = jnp.zeros((HALO, size_y, size_z), F32)
+            courant[pl.ds((planes + HALO) * side, HALO)] = nothing
+            for slot in range(2):
+                field[slot, pl.ds((planes + HALO) * side, HALO)] = nothing
+                for piece in range(2):
+                    wave[slot, pl.ds((planes + deep) * side + HALO * piece, HALO)] = nothing
+
     lax.fori_loop(0, slabs, find_own, 0)
 
     plane_cells = size_y * size_z
@@ -366,51 +396,58 @@
 
     loads[3].wait()
 
+    pair = 2
+
     def adjoint_step(turn, carry):
         slot = lax.rem(turn, 2)
-        data = residual[0, pl.ds(turn, 1)]
-        data_high, data_low = split(data)
+        data_high, data_low = split(residual[turn])
         data_high = data_high.astype(F32)
         data_low = data_low.astype(F32)
-        hot = col_hot[...]
-
-        def advance(index):
-            part = pl.ds(chunk * index, chunk)
-            padded = pl.ds(HALO + chunk * index, chunk)
+
+        def task(number, carry):
+            index = pick(number, order)
+
+            @pl.when(number < 2)
+            def _():
+                adj_wait(slot, number)
+
+            hot = col_hot[...]
             row = lax.broadcasted_iota(jnp.int32, (chunk * size_y, count), 0) + (
                 chunk * size_y * index
             )
             hit = row == recv_row
-            total = lax.dot_general(
-                jnp.where(hit, data_high, 0.0).astype(BF16),
-                hot,
-                (((1,), (1,)), ((), ())),
-                preferred_element_type=F32,
-            )
-            total += lax.dot_general(
-                jnp.where(hit, data_low, 0.0).astype(BF16),
-                hot,
-                (((1,), (1,)), ((), ())),
-                preferred_element_type=F32,
-            )
-            total = total.reshape(chunk, size_y, size_z) + stencil(
-                field, slot, HALO + chunk * index
-            )
-            current = adj[turn + 1, part]
-            following = (current + current) - adj[turn, part] + total
-            adj[turn + 2, part] = following
-            field[1 - slot, padded] = courant[padded] * following
-
-        for side, index in enumerate(edges):
-            adj_wait(slot, side)
-            advance(index)
-
-            @pl.when(turn < ADJ - 1)
+            total = flat_part(field, slot, HALO + chunk * index)
+            for data in (data_high, data_low):
+                total += lax.dot_general(
+                    jnp.where(hit, data, 0.0).astype(BF16),
+                    hot,
+                    (((1,), (1,)), ((), ())),
+                    preferred_element_type=F32,
+                )
+            sums[...] = total.reshape(chunk, size_y, size_z)
+
+            def some(part, carry):
+                plane = chunk * index + pair * part
+                here = pl.ds(plane, pair)
+                padded = pl.ds(HALO + plane, pair)
+                total = sums[pl.ds(pair * part, pair)] + deep_part(
+                    field, slot, HALO + plane, pair
+                )
+                current = adj[turn + 1, here]
+                following = (current + current) - adj[turn, here] + total
+                adj[turn + 2, here] = following
+                field[1 - slot, padded] = courant[padded] * following
+                return carry
+
+            lax.fori_loop(0, chunk // pair, some, 0)
+
+            @pl.when(jnp.logical_and(number < 2, turn < ADJ - 1))
             def _():
-                adj_start(field[1 - slot, pl.ds(HALO + chunk * index, chunk)], 1 - slot, side)
-
-        for index in inner:
-            advance(index)
+                adj_start(index, 1 - slot, number)
+
+            return carry
+
+        lax.fori_loop(0, chunks, task, 0)
         return carry
 
     lax.fori_loop(0, ADJ - 1, adjoint_step, 0)
@@ -426,111 +463,62 @@
 
     def unpack(slab, carry):
         wave[0, deep + slab] = landed_new[own_slots[slab]].astype(F32)
+        wave[1, deep + slab] = jnp.zeros((size_y, size_z), F32)
+        image[slab] = jnp.zeros((size_y, size_z), F32)
         return carry
 
     lax.fori_loop(0, slabs, unpack, 0)
-    for side in range(2):
+
+    def first_edges(side, carry):
         wave_start(0, 0, side, 0)
+        return carry
+
+    lax.fori_loop(0, 2, first_edges, 0)
 
     steps = window_end[0] - snap_step[0]
     start = snap_step[0]
 
-    def image_term(level, turn, index):
+    def image_term(level, turn, plane, width):
         behind = steps - turn
         weight = jnp.where(jnp.logical_and(behind >= 0, behind < ADJ), 1.0, 0.0)
-        state = adj[1 + jnp.clip(behind, 0, ADJ - 1), pl.ds(chunk * index, chunk)]
-        return (weight * state) * wave[level, pl.ds(deep + chunk * index, chunk)]
-
-    def image_add(level, turn):
-        for index in range(chunks):
-            part = pl.ds(chunk * index, chunk)
-            image[part] = image[part] + image_term(level, turn, index)
-
-    def advance(level, turn, index, older=True):
+        state = adj[1 + jnp.clip(behind, 0, ADJ - 1), pl.ds(plane, width)]
+        return (weight * state) * wave[level, pl.ds(deep + plane, width)]
+
+    def advance(level, turn, index):
         first = deep + chunk * index
-        here = pl.ds(first, chunk)
-        middle = wave[level, here]
-        total = courant[pl.ds(first - HALO, chunk)] * stencil(wave, level, first)
-        total = total + (middle + middle)
-        if older:
-            total = total - wave[1 - level, here]
+        sums[...] = flat_part(wave, level, first).reshape(chunk, size_y, size_z)
         amplitude = wavelet[start + turn]
-        pattern = spot[...]
-        for plane in range(chunk):
-            push = jnp.where(source_plane == chunk * index + plane, amplitude, 0.0)
-            wave[1 - level, first + plane] = total[plane] + push * pattern
-
-    for index in inner:
-        advance(0, 0, index, older=False)
-    for index in range(chunks):
-        image[pl.ds(chunk * index, chunk)] = image_term(0, 0, index)
-    adjoint_step(ADJ - 1, 0)
-    result = pltpu.make_async_copy(adj.at[ADJ + 1], adjoint_out, out_sem.at[0])
-    result.start()
-    for side, index in enumerate(edges):
-        wave_wait(0, 0, side, 0)
-        advance(0, 0, index, older=False)
-    arrive(0)
-
-    def less(slab, carry):
-        here = deep + slab
-        wave[1, here] = wave[1, here] - landed_old[own_slots[slab]].astype(F32)
-        return carry
-
-    half = planes // 2
-    for side in range(2):
-        lax.fori_loop(half * side, half * (side + 1), less, 0)
-        for piece in range(2):
-            wave_start(1, 1, side, piece)
-
-    for side in range(2):
-
-        @pl.when(has_side[side])
-        def _():
-            courant_copy(side).wait_send()
-            courant_copy(1 - side).wait_recv()
-            part = pl.ds((planes + HALO) * side, HALO)
-            courant[part] = courant[part] * (1.0 / SCALE)
-
-    blocks = (FWD - 2) // 2
-
-    def block(number, carry):
-        turn = 1 + 2 * number
-        slot = lax.rem(number + 1, 2)
-        for index in inner:
-            advance(1, turn, index)
-        image_add(1, turn)
-        for side in range(2):
-            order = (0, 1) if side == 0 else (chunks - 1, chunks - 2)
-            outside = -1 if side == 0 else chunks
-            wave_wait(1, slot, side, 0)
-            advance(1, turn, order[0])
-            wave_wait(1, slot, side, 1)
-            advance(1, turn, outside)
-            advance(0, turn + 1, order[0])
-            wave_start(1, 1 - slot, side, 0)
-            advance(0, turn + 1, order[1])
-
-            @pl.when(number < blocks - 1)
-            def _():
-                wave_start(1, 1 - slot, side, 1)
-
-        image_add(0, turn + 1)
-        return carry
-
-    lax.fori_loop(0, blocks, block, 0)
+
+        def some(part, carry):
+            at = first + pair * part
+            here = pl.ds(at, pair)
+            middle = wave[level, here]
+            total = sums[pl.ds(pair * part, pair)] + deep_part(wave, level, at, pair)
+            total = courant[pl.ds(at - HALO, pair)] * total
+            total = total + (middle + middle) - wave[1 - level, here]
+            pattern = spot[...]
+            for plane in range(pair):
+                push = jnp.where(source_plane == at - deep + plane, amplitude, 0.0)
+                wave[1 - level, at + plane] = total[plane] + push * pattern
+            return carry
+
+        lax.fori_loop(0, chunk // pair, some, 0)
 
     rows = size_y // chips
     row_half = rows // 2
 
     def cut_image(piece, place_in, index):
-        value = image[pl.ds(chunk * index, chunk)] + image_term(0, FWD, index)
-        for target in range(chips):
-            for side in range(2):
-                low = target * rows + side * row_half
-                split_image[side, piece, target, pl.ds(chunk * place_in, chunk)] = value[
-                    :, low : low + row_half
-                ]
+        def some(part, carry):
+            plane = chunk * index + pair * part
+            value = image[pl.ds(plane, pair)] + image_term(0, FWD, plane, pair)
+            into = pl.ds(chunk * place_in + pair * part, pair)
+            for target in range(chips):
+                for side in range(2):
+                    low = target * rows + side * row_half
+                    split_image[side, piece, target, into] = value[:, low : low + row_half]
+            return carry
+
+        lax.fori_loop(0, chunk // pair, some, 0)
 
     def core_copy(piece):
         return pltpu.make_async_remote_copy(
@@ -564,24 +552,95 @@
         lax.fori_loop(1, chips, one, 0)
         to_chip[piece, chip] = split_image[core, piece, chip] + from_core[piece, chip]
 
-    for index in inner:
-        advance(1, FWD - 1, index)
-    for order, index in enumerate(inner):
-        image[pl.ds(chunk * index, chunk)] = image[pl.ds(chunk * index, chunk)] + image_term(
-            1, FWD - 1, index
-        )
-        cut_image(0, order, index)
-    core_copy(0).start()
-    for index in edges:
-        image[pl.ds(chunk * index, chunk)] = image[pl.ds(chunk * index, chunk)] + image_term(
-            1, FWD - 1, index
-        )
-    to_chips(0)
-    last_slot = (blocks + 1) % 2
-    for side, index in enumerate(edges):
-        wave_wait(1, last_slot, side, 0)
-        advance(1, FWD - 1, index)
-        cut_image(1, side, index)
+    stages = 2 + (FWD - 2) // 2
+
+    def stage(number, carry):
+        opening = number == 0
+        closing = number == stages - 1
+        level = jnp.where(opening, 0, 1)
+        turn = jnp.where(opening, 0, 2 * number - 1)
+        slot = lax.rem(number, 2)
+
+        @pl.when(number > 0)
+        def _():
+            def add_terms(part, carry):
+                plane = pair * part
+                image[pl.ds(plane, pair)] = (
+                    image[pl.ds(plane, pair)]
+                    + image_term(1, turn, plane, pair)
+                    + image_term(0, turn - 1, plane, pair)
+                )
+                return carry
+
+            lax.fori_loop(0, planes // pair, add_terms, 0)
+
+        def task(at, carry):
+            index = pick(at, (1, 2, 0, 3, -1, 0, 1, 4, 3, 2))
+            second = pick(at, (0, 0, 0, 0, 0, 1, 1, 0, 1, 1))
+            side = pick(at, (0, 0, 0, 1, 0, 0, 0, 1, 1, 1))
+            piece = pick(at, (0, 0, 0, 0, 1, 0, 1, 1, 0, 1))
+            waits = pick(at, (0, 0, 1, 1, 1, 0, 0, 1, 0, 0))
+
+            @pl.when(waits == 1)
+            def _():
+                wave_wait(level, slot, side, piece)
+
+            source = jnp.where(second == 1, 1 - level, level)
+            advance(source, turn + second, index)
+
+            @pl.when(
+                jnp.logical_and(second == 1, jnp.logical_or(piece == 0, number < stages - 2))
+            )
+            def _():
+                wave_start(1, 1 - slot, side, piece)
+
+            @pl.when(closing)
+            def _():
+                cut_image(jnp.where(at < 2, 0, 1), lax.rem(at, 2), index)
+
+            @pl.when(jnp.logical_and(closing, at == 1))
+            def _():
+                core_copy(0).start()
+
+            @pl.when(jnp.logical_and(closing, at == 2))
+            def _():
+                to_chips(0)
+
+            return carry
+
+        single = jnp.logical_or(opening, closing)
+        lax.fori_loop(0, jnp.where(single, 4, 10), task, 0)
+
+        @pl.when(opening)
+        def _():
+            arrive(0)
+
+            def less(slab, carry):
+                here = deep + slab
+                wave[1, here] = wave[1, here] - landed_old[own_slots[slab]].astype(F32)
+                return carry
+
+            lax.fori_loop(0, slabs, less, 0)
+
+            def edge(at, carry):
+                wave_start(1, 1, lax.rem(at, 2), lax.div(at, 2))
+                return carry
+
+            lax.fori_loop(0, 4, edge, 0)
+            adjoint_step(ADJ - 1, 0)
+            pltpu.make_async_copy(adj.at[ADJ + 1], adjoint_out, out_sem.at[0]).start()
+            for side in range(2):
+
+                @pl.when(has_side[side])
+                def _():
+                    courant_copy(side).wait_send()
+                    courant_copy(1 - side).wait_recv()
+                    part = pl.ds((planes + HALO) * side, HALO)
+                    courant[part] = courant[part] * (1.0 / SCALE)
+
+        return carry
+
+    lax.fori_loop(0, stages, stage, 0)
     core_copy(1).start()
     to_chips(1)
 
@@ -596,8 +655,8 @@
 
         lax.fori_loop(1, chips, add, 0)
         total = to_chip[piece, chip]
-        for order, index in enumerate((inner, edges)[piece]):
-            image_out[pl.ds(chunk * index, chunk)] = total[chunk * order : chunk * (order + 1)]
+        for at, index in enumerate((inner, edges)[piece]):
+            image_out[pl.ds(chunk * index, chunk)] = total[chunk * at : chunk * (at + 1)]
 
     def drain(turn, carry):
         other = lax.rem(me + turn, shots)
@@ -606,7 +665,16 @@
         return carry
 
     lax.fori_loop(1, shots, drain, 0)
-    result.wait()
+    pltpu.make_async_copy(adj.at[ADJ + 1], adjoint_out, out_sem.at[0]).wait()
+
+
+def finish(image, adjoint, image_out, adjoint_out, sem):
+    copy = pltpu.make_async_copy(adjoint, adjoint_out.at[0], sem.at[0])
+    copy.start()
+    size_z = image.shape[2]
+    for row in range(image.shape[1]):
+        image_out[:, row * size_z : (row + 1) * size_z] = image[:, row] * (1.0 / ADJ)
+    copy.wait()
 
 
 def local(
@@ -660,6 +728,7 @@
             pltpu.VMEM((HALO * size_y, HALO * size_y), BF16),
             pltpu.VMEM((size_y, size_z), F32),
             pltpu.VMEM((size_z, receiver_cells.shape[1]), BF16),
+            pltpu.VMEM((HALO, size_y, size_z), F32),
             pltpu.VMEM((planes, size_y, size_z), F32),
             pltpu.VMEM((2, 2, chips, half, rows // 2, size_z), F32),
             pltpu.VMEM((2, chips, half, rows // 2, size_z), F32),
@@ -692,13 +761,23 @@
         source_cell,
         wavelet,
         receiver_cells,
-        residual_data,
+        residual_data.transpose(1, 0, 2),
         courant,
         snapshot_store.reshape(slabs, 2, size_y, size_z),
         adjoint_prev[0],
         adjoint_now[0],
     )
-    return (image * (1.0 / ADJ)).reshape(planes, rows // 2 * size_z), adjoint[None]
+    return pl.pallas_call(
+        finish,
+        out_shape=(
+            jax.ShapeDtypeStruct((planes, rows // 2 * size_z), F32),
+            jax.ShapeDtypeStruct((1, planes, size_y, size_z), F32),
+        ),
+        in_specs=[vmem, hbm],
+        out_specs=(vmem, hbm),
+        scratch_shapes=[dma((1,))],
+        compiler_params=pltpu.CompilerParams(vmem_limit_bytes=63 * 2**20),
+    )(image, adjoint)
 
 
 def solution(mesh):

time: 109 us -> 138 us (1.27)
  Pallas kernels: 101 us -> 135 us
  local copies, waits for them, and re-layouts: 4.21 us -> 0 us
    pallas_call x0 -> x1, Pallas kernels: none -> 34.3 us  [local(): pl.pallas_call(finish, out_shape=(jax.ShapeDtypeStruct((planes, rows // 2...]
    unnamed x5 -> x0, local copies, waits for them, and re-layouts: 4.21 us -> none
where the time goes in v2:
time: 138 us
  Pallas kernels  135 us (98%)
  between operations  2.58 us (2%)
    pallas_call x1, Pallas kernels, local(): pl.pallas_call(functools.partial(kernel, shots, spaces, cap), out_shape=(...  101 us
    pallas_call x1, Pallas kernels, local(): pl.pallas_call(finish, out_shape=(jax.ShapeDtypeStruct((planes, rows // 2...  34.3 us

profile of v2, /device:TPU:248, one launch (start us, length us, event | category | flops | bytes accessed | tf_op | source)
XLA Modules:
  0.0 137.7 jit_solution(11476867933548184419)
XLA Ops:
  2.6 100.8 %shard_map.122 = (f32[16,4,256]{2,1,0:T(4,128)}, f32[16,64,256]{2,1,0:T(8,128)}) custom-call(s32[16,16]{1,0:T(8,128)} %holder.1, s32[1]{0:T(128)S(6)} %copy.13.snap_step, s32[1]{0:T(128)S(6)} %copy.14.window_end, s32[1]{0:T(128)S(6)} %copy.15.source_cell, f32[64]{0:T(128)} %wavelet.1, s32[1,256]{1,0:T(1,128)} %cells.1, f32[3,1,256]{2,1,0:T(1,128)} %bitcast.7, ...), custom_call_target="tpu_custom_call" | custom-call | tf_op jit(solution)/shard_map/pallas_call | solution.py:706
  103.4 34.3 %shard_map.123 = (f32[16,1024]{1,0:T(8,128)}, f32[1,16,64,256]{3,2,1,0:T(8,128)}) custom-call(f32[16,4,256]{2,1,0:T(4,128)} %get-tuple-element.4.image, f32[16,64,256]{2,1,0:T(8,128)} %get-tuple-element.5.adjoint), custom_call_target="tpu_custom_call" | custom-call | tf_op jit(solution)/shard_map/pallas_call | solution.py:770

commit v3 on v2

--- a/solution.py
+++ b/solution.py
@@ -87,7 +87,6 @@
     band_y,
     spot,
     col_hot,
-    sums,
     image,
     split_image,
     from_core,
@@ -271,7 +270,7 @@
             side,
         )
 
-    def flat_part(ref, slot, first):
+    def stencil(ref, slot, first):
         middle = ref[slot, pl.ds(first, chunk)]
         high, low = split(middle.reshape(chunk * size_y, size_z))
         right = band_z[...]
@@ -280,13 +279,11 @@
         total += jnp.dot(low, right, preferred_element_type=F32)
         total += jnp.dot(left, high, preferred_element_type=F32)
         total += jnp.dot(left, low, preferred_element_type=F32)
-        return total
-
-    def deep_part(ref, slot, at, width):
-        total = None
+        total = total.reshape(chunk, size_y, size_z)
         for offset, tap in enumerate(TAPS, 1):
-            term = tap * (ref[slot, pl.ds(at + offset, width)] + ref[slot, pl.ds(at - offset, width)])
-            total = term if total is None else total + term
+            total += tap * (
+                ref[slot, pl.ds(first + offset, chunk)] + ref[slot, pl.ds(first - offset, chunk)]
+            )
         return total
 
     order = (0, chunks - 1) + inner
@@ -404,19 +401,13 @@
         data_high = data_high.astype(F32)
         data_low = data_low.astype(F32)
 
-        def task(number, carry):
-            index = pick(number, order)
-
-            @pl.when(number < 2)
-            def _():
-                adj_wait(slot, number)
-
+        def work(index):
             hot = col_hot[...]
             row = lax.broadcasted_iota(jnp.int32, (chunk * size_y, count), 0) + (
                 chunk * size_y * index
             )
             hit = row == recv_row
-            total = flat_part(field, slot, HALO + chunk * index)
+            total = jnp.zeros((chunk * size_y, size_z), F32)
             for data in (data_high, data_low):
                 total += lax.dot_general(
                     jnp.where(hit, data, 0.0).astype(BF16),
@@ -424,33 +415,30 @@
                     (((1,), (1,)), ((), ())),
                     preferred_element_type=F32,
                 )
-            sums[...] = total.reshape(chunk, size_y, size_z)
-
-            def some(part, carry):
-                plane = chunk * index + pair * part
-                here = pl.ds(plane, pair)
-                padded = pl.ds(HALO + plane, pair)
-                total = sums[pl.ds(pair * part, pair)] + deep_part(
-                    field, slot, HALO + plane, pair
-                )
-                current = adj[turn + 1, here]
-                following = (current + current) - adj[turn, here] + total
-                adj[turn + 2, here] = following
-                field[1 - slot, padded] = courant[padded] * following
-                return carry
-
-            lax.fori_loop(0, chunk // pair, some, 0)
-
-            @pl.when(jnp.logical_and(number < 2, turn < ADJ - 1))
+            total = total.reshape(chunk, size_y, size_z)
+            total = total + stencil(field, slot, HALO + chunk * index)
+            here = pl.ds(chunk * index, chunk)
+            padded = pl.ds(HALO + chunk * index, chunk)
+            current = adj[turn + 1, here]
+            following = (current + current) - adj[turn, here] + total
+            adj[turn + 2, here] = following
+            field[1 - slot, padded] = courant[padded] * following
+
+        def task(side, carry):
+            adj_wait(slot, side)
+            index = (chunks - 1) * side
+            work(index)
+
+            @pl.when(turn < ADJ - 1)
             def _():
-                adj_start(index, 1 - slot, number)
+                adj_start(index, 1 - slot, side)
 
             return carry
 
-        lax.fori_loop(0, chunks, task, 0)
-        return carry
-
-    lax.fori_loop(0, ADJ - 1, adjoint_step, 0)
+        lax.fori_loop(0, 2, task, 0)
+        for index in inner:
+            work(index)
+        return carry
 
     def arrive(level):
         def one(turn, carry):
@@ -459,21 +447,28 @@
 
         lax.fori_loop(1, shots, one, 0)
 
-    arrive(1)
-
     def unpack(slab, carry):
         wave[0, deep + slab] = landed_new[own_slots[slab]].astype(F32)
         wave[1, deep + slab] = jnp.zeros((size_y, size_z), F32)
         image[slab] = jnp.zeros((size_y, size_z), F32)
         return carry
 
-    lax.fori_loop(0, slabs, unpack, 0)
-
     def first_edges(side, carry):
         wave_start(0, 0, side, 0)
         return carry
 
-    lax.fori_loop(0, 2, first_edges, 0)
+    def early(turn, carry):
+        adjoint_step(turn, 0)
+
+        @pl.when(turn == 0)
+        def _():
+            arrive(1)
+            lax.fori_loop(0, slabs, unpack, 0)
+            lax.fori_loop(0, 2, first_edges, 0)
+
+        return carry
+
+    lax.fori_loop(0, ADJ - 1, early, 0)
 
     steps = window_end[0] - snap_step[0]
     start = snap_step[0]
@@ -486,23 +481,15 @@
 
     def advance(level, turn, index):
         first = deep + chunk * index
-        sums[...] = flat_part(wave, level, first).reshape(chunk, size_y, size_z)
+        here = pl.ds(first, chunk)
+        middle = wave[level, here]
+        total = courant[pl.ds(first - HALO, chunk)] * stencil(wave, level, first)
+        total = total + (middle + middle) - wave[1 - level, here]
         amplitude = wavelet[start + turn]
-
-        def some(part, carry):
-            at = first + pair * part
-            here = pl.ds(at, pair)
-            middle = wave[level, here]
-            total = sums[pl.ds(pair * part, pair)] + deep_part(wave, level, at, pair)
-            total = courant[pl.ds(at - HALO, pair)] * total
-            total = total + (middle + middle) - wave[1 - level, here]
-            pattern = spot[...]
-            for plane in range(pair):
-                push = jnp.where(source_plane == at - deep + plane, amplitude, 0.0)
-                wave[1 - level, at + plane] = total[plane] + push * pattern
-            return carry
-
-        lax.fori_loop(0, chunk // pair, some, 0)
+        pattern = spot[...]
+        for plane in range(chunk):
+            push = jnp.where(source_plane == chunk * index + plane, amplitude, 0.0)
+            wave[1 - level, first + plane] = total[plane] + push * pattern
 
     rows = size_y // chips
     row_half = rows // 2
@@ -574,12 +561,24 @@
 
             lax.fori_loop(0, planes // pair, add_terms, 0)
 
+        for index in inner:
+            advance(level, turn, index)
+
+        @pl.when(closing)
+        def _():
+            def one(at, carry):
+                cut_image(0, at, 1 + at)
+                return carry
+
+            lax.fori_loop(0, len(inner), one, 0)
+            core_copy(0).start()
+
         def task(at, carry):
-            index = pick(at, (1, 2, 0, 3, -1, 0, 1, 4, 3, 2))
-            second = pick(at, (0, 0, 0, 0, 0, 1, 1, 0, 1, 1))
-            side = pick(at, (0, 0, 0, 1, 0, 0, 0, 1, 1, 1))
-            piece = pick(at, (0, 0, 0, 0, 1, 0, 1, 1, 0, 1))
-            waits = pick(at, (0, 0, 1, 1, 1, 0, 0, 1, 0, 0))
+            index = pick(at, (0, 3, -1, 0, 1, 4, 3, 2))
+            second = pick(at, (0, 0, 0, 1, 1, 0, 1, 1))
+            side = pick(at, (0, 1, 0, 0, 0, 1, 1, 1))
+            piece = pick(at, (0, 0, 1, 0, 1, 1, 0, 1))
+            waits = pick(at, (1, 1, 1, 0, 0, 1, 0, 0))
 
             @pl.when(waits == 1)
             def _():
@@ -596,20 +595,16 @@
 
             @pl.when(closing)
             def _():
-                cut_image(jnp.where(at < 2, 0, 1), lax.rem(at, 2), index)
-
-            @pl.when(jnp.logical_and(closing, at == 1))
-            def _():
-                core_copy(0).start()
-
-            @pl.when(jnp.logical_and(closing, at == 2))
+                cut_image(1, at, index)
+
+            @pl.when(jnp.logical_and(closing, at == 0))
             def _():
                 to_chips(0)
 
             return carry
 
         single = jnp.logical_or(opening, closing)
-        lax.fori_loop(0, jnp.where(single, 4, 10), task, 0)
+        lax.fori_loop(0, jnp.where(single, 2, 8), task, 0)
 
         @pl.when(opening)
         def _():
@@ -668,13 +663,16 @@
     pltpu.make_async_copy(adj.at[ADJ + 1], adjoint_out, out_sem.at[0]).wait()
 
 
-def finish(image, adjoint, image_out, adjoint_out, sem):
-    copy = pltpu.make_async_copy(adjoint, adjoint_out.at[0], sem.at[0])
-    copy.start()
+def finish(image, adjoint, image_out, adjoint_out):
     size_z = image.shape[2]
     for row in range(image.shape[1]):
         image_out[:, row * size_z : (row + 1) * size_z] = image[:, row] * (1.0 / ADJ)
-    copy.wait()
+
+    def one(plane, carry):
+        adjoint_out[0, plane] = adjoint[plane]
+        return carry
+
+    lax.fori_loop(0, adjoint.shape[0], one, 0)
 
 
 def local(
@@ -728,7 +726,6 @@
             pltpu.VMEM((HALO * size_y, HALO * size_y), BF16),
             pltpu.VMEM((size_y, size_z), F32),
             pltpu.VMEM((size_z, receiver_cells.shape[1]), BF16),
-            pltpu.VMEM((HALO, size_y, size_z), F32),
             pltpu.VMEM((planes, size_y, size_z), F32),
             pltpu.VMEM((2, 2, chips, half, rows // 2, size_z), F32),
             pltpu.VMEM((2, chips, half, rows // 2, size_z), F32),
@@ -773,10 +770,9 @@
             jax.ShapeDtypeStruct((planes, rows // 2 * size_z), F32),
             jax.ShapeDtypeStruct((1, planes, size_y, size_z), F32),
         ),
-        in_specs=[vmem, hbm],
-        out_specs=(vmem, hbm),
-        scratch_shapes=[dma((1,))],
-        compiler_params=pltpu.CompilerParams(vmem_limit_bytes=63 * 2**20),
+        in_specs=[vmem, vmem],
+        out_specs=(vmem, vmem),
+        compiler_params=pltpu.CompilerParams(vmem_limit_bytes=16 * 2**20),
     )(image, adjoint)
 
 

time: 138 us -> 111 us (0.80)
  Pallas kernels: 135 us -> 106 us
  local copies, waits for them, and re-layouts: 0 us -> 2.06 us
    pallas_call x1, Pallas kernels: 34.3 us -> 1.13 us  [local(): pl.pallas_call(finish, out_shape=(jax.ShapeDtypeStruct((planes, rows // 2...]
    pallas_call x1, Pallas kernels: 101 us -> 105 us  [local(): pl.pallas_call(functools.partial(kernel, shots, spaces, cap), out_shape=(...]
    unnamed x0 -> x4, local copies, waits for them, and re-layouts: none -> 2.06 us
where the time goes in v3:
time: 111 us
  Pallas kernels  106 us (95%)
  between operations  2.59 us (2%)
  local copies, waits for them, and re-layouts  2.06 us (2%)
    pallas_call x1, Pallas kernels, local(): pl.pallas_call(functools.partial(kernel, shots, spaces, cap), out_shape=(...  105 us

profile of v3, /device:TPU:248, one launch (start us, length us, event | category | flops | bytes accessed | tf_op | source)
XLA Modules:
  0.0 111.1 jit_solution(1692689218179079140)
XLA Ops:
  2.6 105.3 %shard_map.122 = (f32[16,4,256]{2,1,0:T(4,128)}, f32[16,64,256]{2,1,0:T(8,128)}) custom-call(s32[16,16]{1,0:T(8,128)} %holder.1, s32[1]{0:T(128)S(6)} %copy.13.snap_step, s32[1]{0:T(128)S(6)} %copy.14.window_end, s32[1]{0:T(128)S(6)} %copy.15.source_cell, f32[64]{0:T(128)} %wavelet.1, s32[1,256]{1,0:T(1,128)} %cells.1, f32[3,1,256]{2,1,0:T(1,128)} %bitcast.7, ...), custom_call_target="tpu_custom_call" | custom-call | tf_op jit(solution)/shard_map/pallas_call | solution.py:704
  107.9 0.0 copy-start
  107.9 1.2 %copy-done = f32[16,64,256]{2,1,0:T(8,128)S(1)} copy-done((f32[16,64,256]{2,1,0:T(8,128)S(1)}, f32[16,64,256]{2,1,0:T(8,128)}, u32[]{:S(2)}) %copy-start) | copy-done | bytes 1048600
  109.2 0.0 copy-start.1
  109.2 0.8 copy-done.1
  110.0 1.1 %shard_map.123 = (f32[16,1024]{1,0:T(8,128)}, f32[1,16,64,256]{3,2,1,0:T(8,128)}) custom-call(f32[16,4,256]{2,1,0:T(4,128)S(1)} %copy-done.1, f32[16,64,256]{2,1,0:T(8,128)S(1)} %copy-done), custom_call_target="tpu_custom_call" | custom-call | tf_op jit(solution)/shard_map/pallas_call | solution.py:767
Async XLA Ops:
  107.9 1.2 %copy-start = (f32[16,64,256]{2,1,0:T(8,128)S(1)}, f32[16,64,256]{2,1,0:T(8,128)}, u32[]{:S(2)}) copy-start(f32[16,64,256]{2,1,0:T(8,128)} %get-tuple-element.5.adjoint) | copy-start | bytes 3145732
  109.2 0.8 copy-start.1

commit v4 on v3

--- a/solution.py
+++ b/solution.py
@@ -393,7 +393,7 @@
 
     loads[3].wait()
 
-    pair = 2
+    pair = 4
 
     def adjoint_step(turn, carry):
         slot = lax.rem(turn, 2)
@@ -457,18 +457,10 @@
         wave_start(0, 0, side, 0)
         return carry
 
-    def early(turn, carry):
-        adjoint_step(turn, 0)
-
-        @pl.when(turn == 0)
-        def _():
-            arrive(1)
-            lax.fori_loop(0, slabs, unpack, 0)
-            lax.fori_loop(0, 2, first_edges, 0)
-
-        return carry
-
-    lax.fori_loop(0, ADJ - 1, early, 0)
+    lax.fori_loop(0, ADJ - 1, adjoint_step, 0)
+    arrive(1)
+    lax.fori_loop(0, slabs, unpack, 0)
+    lax.fori_loop(0, 2, first_edges, 0)
 
     steps = window_end[0] - snap_step[0]
     start = snap_step[0]
@@ -772,7 +764,7 @@
         ),
         in_specs=[vmem, vmem],
         out_specs=(vmem, vmem),
-        compiler_params=pltpu.CompilerParams(vmem_limit_bytes=16 * 2**20),
+        compiler_params=pltpu.CompilerParams(vmem_limit_bytes=63 * 2**20),
     )(image, adjoint)
 
 

time: 111 us -> 105 us (0.946)
  Pallas kernels: 106 us -> 102 us
  local copies, waits for them, and re-layouts: 2.06 us -> 0 us
    pallas_call x1, Pallas kernels: 105 us -> 99.4 us  [local(): pl.pallas_call(functools.partial(kernel, shots, spaces, cap), out_shape=(...]
    unnamed x4 -> x0, local copies, waits for them, and re-layouts: 2.06 us -> none
    pallas_call x1, Pallas kernels: 1.13 us -> 2.39 us  [local(): pl.pallas_call(finish, out_shape=(jax.ShapeDtypeStruct((planes, rows // 2...]
where the time goes in v4:
time: 105 us; the launch traced here: 104 us
  Pallas kernels  102 us (97%)
  between operations  2.58 us (2%)
    pallas_call x1, Pallas kernels, local(): pl.pallas_call(functools.partial(kernel, shots, spaces, cap), out_shape=(...  99.4 us
    pallas_call x1, Pallas kernels, local(): pl.pallas_call(finish, out_shape=(jax.ShapeDtypeStruct((planes, rows // 2...  2.39 us

profile of v4, /device:TPU:248, one launch (start us, length us, event | category | flops | bytes accessed | tf_op | source)
XLA Modules:
  0.0 104.3 jit_solution(6670237859095105612)
XLA Ops:
  2.6 99.4 %shard_map.122 = (f32[16,4,256]{2,1,0:T(4,128)}, f32[16,64,256]{2,1,0:T(8,128)}) custom-call(s32[16,16]{1,0:T(8,128)} %holder.1, s32[1]{0:T(128)S(6)} %copy.13.snap_step, s32[1]{0:T(128)S(6)} %copy.14.window_end, s32[1]{0:T(128)S(6)} %copy.15.source_cell, f32[64]{0:T(128)} %wavelet.1, s32[1,256]{1,0:T(1,128)} %cells.1, f32[3,1,256]{2,1,0:T(1,128)} %bitcast.7, ...), custom_call_target="tpu_custom_call" | custom-call | tf_op jit(solution)/shard_map/pallas_call | solution.py:696
  101.9 2.4 %shard_map.123 = (f32[16,1024]{1,0:T(8,128)}, f32[1,16,64,256]{3,2,1,0:T(8,128)}) custom-call(f32[16,4,256]{2,1,0:T(4,128)} %get-tuple-element.4.image, f32[16,64,256]{2,1,0:T(8,128)} %get-tuple-element.5.adjoint), custom_call_target="tpu_custom_call" | custom-call | tf_op jit(solution)/shard_map/pallas_call | solution.py:759

commit v5 on v4

--- a/solution.py
+++ b/solution.py
@@ -288,6 +288,12 @@
 
     order = (0, chunks - 1) + inner
 
+    odd = lax.rem(place, 2)
+
+    def mirror(side):
+        return side + odd * (1 - 2 * side)
+
+
     def first_field(turn, carry):
         index = pick(turn, order)
         part = pl.ds(HALO + chunk * index, chunk)
@@ -424,7 +430,8 @@
             adj[turn + 2, here] = following
             field[1 - slot, padded] = courant[padded] * following
 
-        def task(side, carry):
+        def task(at, carry):
+            side = mirror(at)
             adj_wait(slot, side)
             index = (chunks - 1) * side
             work(index)
@@ -453,8 +460,8 @@
         image[slab] = jnp.zeros((size_y, size_z), F32)
         return carry
 
-    def first_edges(side, carry):
-        wave_start(0, 0, side, 0)
+    def first_edges(at, carry):
+        wave_start(0, 0, mirror(at), 0)
         return carry
 
     lax.fori_loop(0, ADJ - 1, adjoint_step, 0)
@@ -567,8 +574,9 @@
 
         def task(at, carry):
             index = pick(at, (0, 3, -1, 0, 1, 4, 3, 2))
+            index = index + odd * (chunks - 1 - 2 * index)
             second = pick(at, (0, 0, 0, 1, 1, 0, 1, 1))
-            side = pick(at, (0, 1, 0, 0, 0, 1, 1, 1))
+            side = mirror(pick(at, (0, 1, 0, 0, 0, 1, 1, 1)))
             piece = pick(at, (0, 0, 1, 0, 1, 1, 0, 1))
             waits = pick(at, (1, 1, 1, 0, 0, 1, 0, 0))
 
@@ -587,7 +595,7 @@
 
             @pl.when(closing)
             def _():
-                cut_image(1, at, index)
+                cut_image(1, mirror(at), index)
 
             @pl.when(jnp.logical_and(closing, at == 0))
             def _():
@@ -610,7 +618,7 @@
             lax.fori_loop(0, slabs, less, 0)
 
             def edge(at, carry):
-                wave_start(1, 1, lax.rem(at, 2), lax.div(at, 2))
+                wave_start(1, 1, mirror(lax.rem(at, 2)), lax.div(at, 2))
                 return carry
 
             lax.fori_loop(0, 4, edge, 0)

time: 105 us -> 105 us (level)
  no operation moved by 1% of the time
where the time goes in v5:
time: 105 us; the launch traced here: 104 us
  Pallas kernels  102 us (97%)
  between operations  2.58 us (2%)
    pallas_call x1, Pallas kernels, local(): pl.pallas_call(functools.partial(kernel, shots, spaces, cap), out_shape=(...  99.4 us
    pallas_call x1, Pallas kernels, local(): pl.pallas_call(finish, out_shape=(jax.ShapeDtypeStruct((planes, rows // 2...  2.39 us

profile of v5, /device:TPU:248, one launch (start us, length us, event | category | flops | bytes accessed | tf_op | source)
XLA Modules:
  0.0 104.4 jit_solution(5152995303032829572)
XLA Ops:
  2.6 99.4 %shard_map.122 = (f32[16,4,256]{2,1,0:T(4,128)}, f32[16,64,256]{2,1,0:T(8,128)}) custom-call(s32[16,16]{1,0:T(8,128)} %holder.1, s32[1]{0:T(128)S(6)} %copy.13.snap_step, s32[1]{0:T(128)S(6)} %copy.14.window_end, s32[1]{0:T(128)S(6)} %copy.15.source_cell, f32[64]{0:T(128)} %wavelet.1, s32[1,256]{1,0:T(1,128)} %cells.1, f32[3,1,256]{2,1,0:T(1,128)} %bitcast.7, ...), custom_call_target="tpu_custom_call" | custom-call | tf_op jit(solution)/shard_map/pallas_call | solution.py:704
  102.0 2.4 %shard_map.123 = (f32[16,1024]{1,0:T(8,128)}, f32[1,16,64,256]{3,2,1,0:T(8,128)}) custom-call(f32[16,4,256]{2,1,0:T(4,128)} %get-tuple-element.4.image, f32[16,64,256]{2,1,0:T(8,128)} %get-tuple-element.5.adjoint), custom_call_target="tpu_custom_call" | custom-call | tf_op jit(solution)/shard_map/pallas_call | solution.py:767
